TPU v7x, 32 devices: a whole 2x2x4 slice. The times are simulated.
32 devices in a mesh: groups: 2 (over x), score: 16 (over z, y, core).
Axes of the slice: x: 2, y: 2, z: 4, core: 2. Of those that a mesh axis runs over, the one named last changes fastest.
Arguments:
- hidden: bfloat16 [4096, 8192], P(('groups', 'score')), parts along dimension 0, may hold values from -6 to 6
- frozen_query_rows: bfloat16 [4096, 4096], P(('groups', 'score')), parts along dimension 0, may hold values from -64 to 64
- answer_row_key: bfloat16 [4096, 512], P(('groups', 'score')), parts along dimension 0, may hold values from -6 to 6
- answer_row_value: bfloat16 [4096, 512], P(('groups', 'score')), parts along dimension 0, may hold values from -6 to 6
- row_request_index: int32 [4096, 1], P(('groups', 'score')), parts along dimension 0, may hold values from 0 to 15; in each aligned block of 128 rows (0 to 127, 128 to 255, ...) at most 12 rows name the same one
- row_checkpoint_index: int32 [4096], P(('groups', 'score')), parts along dimension 0, may hold values from 0 to 7
- request_device_owner: int32 [32], P('groups'), parts along dimension 0, may hold values from 0 to 15, each once
- request_block_table: int32 [32, 12], P('groups'), parts along dimension 0, may hold values from 0 to 11, each once within a row
- request_prefix_length: int32 [32], P('groups'), parts along dimension 0, may hold values from 128 to 1536
- adapter_down_weight: bfloat16 [8192, 512], P('score'), may hold values from -0.0625 to 0.0625
- adapter_up_weight: bfloat16 [4096, 512], P('score'), may hold values from -0.75 to 0.75
- paged_key_blocks: bfloat16 [384, 128, 512], P(('groups', 'score')), parts along dimension 0, may hold values from -8 to 8
- paged_value_blocks: bfloat16 [384, 128, 512], P(('groups', 'score')), parts along dimension 0, may hold values from -6 to 6
Outputs:
- context: bfloat16 [4096, 4096], P(('groups', 'score')), parts along dimension 0
There are 2 independent parts, one for each index of `groups`. A program takes and returns all parts, laid end to end along the dimension named above; an argument that names none is the same for every part. Nothing has to cross between parts.
Inputs may be any that keep to these rules, and one draw needn't show every extreme that they name: `row_request_index`: among the rows of one device at most 12 name the same request; in some device exactly 12 do. `request_device_owner`: each device stores the prefix of exactly one request. `request_block_table`: each request lists every one of its owner's 12 cache slots once, in prefix order.
All inputs are finite; a program needn't handle non-finite values.
Results may differ from a plain program's by a relative error of at most 0.012.
The roundings to bfloat16 on the way count: a program that leaves them out, or rounds other values in their place, can miss the bound.
Values may be sent and summed in bfloat16 or wider, within the bound.
A program may use at most 128 MiB of HBM per device.

v0:
```python
import jax
import jax.numpy as jnp
from jax import lax
from jax.sharding import PartitionSpec as P

QUERY_HEADS = 32
KEY_VALUE_HEADS = 4
HEAD_SIZE = 128
ADAPTER_RANK = 64
BLOCK_TOKENS = 128
MAXB = 12


def self_scores(query_matrix, self_key_rows):
    item_count = query_matrix.shape[0]
    head_group = QUERY_HEADS // KEY_VALUE_HEADS
    head_list = query_matrix.reshape(item_count, KEY_VALUE_HEADS, head_group, HEAD_SIZE)
    keyed_rows = self_key_rows.reshape(item_count, KEY_VALUE_HEADS, HEAD_SIZE)
    scored = jnp.einsum("rhgd,rhd->rhg", head_list, keyed_rows, preferred_element_type=jnp.float32)
    return scored.reshape(item_count, QUERY_HEADS) * (1.0 / HEAD_SIZE**0.5)


def attend_core(query_matrix, own_part, self_value_rows, key_rows, value_rows, live):
    item_count = query_matrix.shape[0]
    head_group = QUERY_HEADS // KEY_VALUE_HEADS
    score_scale = 1.0 / HEAD_SIZE**0.5
    outputs = []
    for head_slice in range(KEY_VALUE_HEADS):
        head_list = query_matrix[
            :, head_slice * head_group * HEAD_SIZE : (head_slice + 1) * head_group * HEAD_SIZE
        ].reshape(item_count, head_group, HEAD_SIZE)
        key_head = key_rows[:, head_slice * HEAD_SIZE : (head_slice + 1) * HEAD_SIZE]
        value_head = value_rows[:, head_slice * HEAD_SIZE : (head_slice + 1) * HEAD_SIZE]
        scores = (
            jnp.einsum("rgd,ld->rgl", head_list, key_head, preferred_element_type=jnp.float32)
            * score_scale
        )
        scores = jnp.where(live[None, None, :], scores, -jnp.inf)
        own_head = own_part[:, head_slice * head_group : (head_slice + 1) * head_group]
        top = jnp.maximum(jnp.max(scores, -1), own_head)
        weights = jnp.exp(scores - top[..., None])
        self_weight = jnp.exp(own_head - top)
        total = jnp.sum(weights, -1) + self_weight
        weights = (weights / total[..., None]).astype(jnp.bfloat16)
        self_weight = (self_weight / total).astype(jnp.bfloat16)
        mixed_output = jnp.einsum(
            "rgl,ld->rgd", weights, value_head, preferred_element_type=jnp.float32
        )
        mixed_output = (
            mixed_output
            + self_weight.astype(jnp.float32)[..., None]
            * self_value_rows[:, head_slice * HEAD_SIZE : (head_slice + 1) * HEAD_SIZE].astype(
                jnp.float32
            )[:, None, :]
        )
        outputs.append(
            mixed_output.reshape(item_count, head_group * HEAD_SIZE).astype(jnp.bfloat16)
        )
    return jnp.concatenate(outputs, 1)


def on_device(
    hidden,
    frozen_query_rows,
    answer_row_key,
    answer_row_value,
    row_request_index,
    row_checkpoint_index,
    request_device_owner,
    request_block_table,
    request_prefix_length,
    adapter_down_weight,
    adapter_up_weight,
    paged_key_blocks,
    paged_value_blocks,
):
    rows = hidden.shape[0]
    devices = lax.axis_size("score")
    capacity = max(2, (3 * rows + 2 * devices - 1) // (2 * devices))
    width = frozen_query_rows.shape[1]
    kv_width = answer_row_key.shape[1]
    token_span = MAXB * BLOCK_TOKENS
    column_list = adapter_down_weight.shape[1]
    column_owner = jnp.arange(column_list, dtype=jnp.int32) // ADAPTER_RANK
    chosen = row_checkpoint_index[:, None] == column_owner[None, :]
    inner_product = jnp.dot(
        hidden,
        lax.all_gather(adapter_down_weight, "score", axis=0, tiled=True),
        preferred_element_type=jnp.float32,
    )
    masked_scores = jnp.where(chosen, inner_product, 0.0).astype(jnp.bfloat16)
    adapter_change = lax.dot_general(
        masked_scores,
        lax.all_gather(adapter_up_weight, "score", axis=0, tiled=True),
        (((1,), (1,)), ((), ())),
        preferred_element_type=jnp.float32,
    )
    query = (frozen_query_rows.astype(jnp.float32) + 2.0 * adapter_change).astype(jnp.bfloat16)
    req_ids = jnp.arange(devices, dtype=jnp.int32)
    requests = row_request_index[:, 0]
    picked = requests[:, None] == req_ids[None, :]
    target = jnp.sum(jnp.where(picked, request_device_owner[None, :], 0), 1)
    hits = (target[:, None] == req_ids[None, :]).astype(jnp.int32)
    before = jnp.cumsum(hits, 0) - hits
    rank_in = jnp.sum(before * hits, 1)
    slot = target * capacity + rank_in

    def place(value_rows):
        filled = (
            jnp.zeros((devices * capacity, value_rows.shape[1]), value_rows.dtype)
            .at[slot]
            .set(value_rows)
        )
        return filled.reshape(devices, capacity, value_rows.shape[1])

    here = lax.axis_index("score")
    local_req = jnp.sum(jnp.where(request_device_owner == here, req_ids, 0))
    order = lax.dynamic_index_in_dim(request_block_table, local_req, 0, keepdims=False)
    length = lax.dynamic_index_in_dim(request_prefix_length, local_req, 0, keepdims=False)
    key_rows = paged_key_blocks[order].reshape(token_span, kv_width)
    value_rows = paged_value_blocks[order].reshape(token_span, kv_width)
    live = jnp.arange(token_span, dtype=jnp.int32) < length
    query_matrix = lax.all_to_all(place(query), "score", split_axis=0, concat_axis=0, tiled=True)
    self_key_rows = lax.all_to_all(
        place(answer_row_key), "score", split_axis=0, concat_axis=0, tiled=True
    )
    self_value_rows = lax.all_to_all(
        place(answer_row_value), "score", split_axis=0, concat_axis=0, tiled=True
    )
    array_shape = query_matrix.shape
    item_count = array_shape[0] * array_shape[1]
    query_matrix = query_matrix.reshape(item_count, width)
    own_part = self_scores(query_matrix, self_key_rows.reshape(item_count, kv_width))
    answer = attend_core(
        query_matrix,
        own_part,
        self_value_rows.reshape(item_count, kv_width),
        key_rows,
        value_rows,
        live,
    )
    returned = lax.all_to_all(
        answer.reshape(array_shape[0], array_shape[1], width),
        "score",
        split_axis=0,
        concat_axis=0,
        tiled=True,
    )
    return returned.reshape(devices * capacity, width)[slot]


def solution(mesh):
    placed = (
        P(("groups", "score"), None),
        P(("groups", "score"), None),
        P(("groups", "score"), None),
        P(("groups", "score"), None),
        P(("groups", "score"), None),
        P(("groups", "score")),
        P("groups"),
        P("groups", None),
        P("groups"),
        P("score", None),
        P("score", None),
        P(("groups", "score"), None, None),
        P(("groups", "score"), None, None),
    )
    return jax.shard_map(
        on_device,
        mesh=mesh,
        in_specs=placed,
        out_specs=P(("groups", "score"), None),
        check_vma=False,
    )
```

profile of v0, /device:TPU:0, one launch (start us, length us, event | category | flops | bytes accessed | tf_op | source)
XLA Modules:
  0.0 346.8 jit_solution(12392494867394743464)
XLA Ops:
  9.3 1.5 scatter_custom_fusion.1
  11.6 7.4 %all-to-all-start.1 = ((bf16[16,12,512]{2,1,0:T(8,128)(2,1)}), bf16[16,12,512]{2,1,0:T(8,128)(2,1)S(1)}, u32[]{:S(2)}, u32[]{:S(2)}) async-start(bf16[16,12,512]{2,1,0:T(8,128)(2,1)} %reshape.150), calls=%async_computation.1 | async-start | bytes 524288 | tf_op jit(solution)/shard_map/all_to_all | solution.py:124
  18.9 1.5 scatter_custom_fusion.2
  21.2 11.4 %all-to-all-done.1 = bf16[16,12,512]{2,1,0:T(8,128)(2,1)S(1)} async-done(((bf16[16,12,512]{2,1,0:T(8,128)(2,1)}), bf16[16,12,512]{2,1,0:T(8,128)(2,1)S(1)}, u32[]{:S(2)}, u32[]{:S(2)}) %all-to-all-start.1) | async-done | bytes 196640 | tf_op jit(solution)/shard_map/all_to_all | solution.py:124
  32.6 4.2 %all-to-all-start.2 = ((bf16[16,12,512]{2,1,0:T(8,128)(2,1)}), bf16[16,12,512]{2,1,0:T(8,128)(2,1)S(1)}, u32[]{:S(2)}, u32[]{:S(2)}) async-start(bf16[16,12,512]{2,1,0:T(8,128)(2,1)} %reshape.152), calls=%async_computation.2 | async-start | bytes 524288 | tf_op jit(solution)/shard_map/all_to_all | solution.py:127
  36.9 30.5 %all-gather.5.cloned.1.call-done = bf16[4096,512]{1,0:T(8,128)(2,1)} async-done(((bf16[256,512]{1,0:T(8,128)(2,1)}), bf16[4096,512]{1,0:T(8,128)(2,1)}) %all-gather.5.cloned.1.call-update) | async-done | bytes 4194320 | tf_op jit(solution)/shard_map/all_gather | solution.py:94
  67.3 75.7 %all-gather.3.cloned.1.call-done = bf16[8192,512]{1,0:T(8,128)(2,1)} async-done(((bf16[512,512]{1,0:T(8,128)(2,1)}), bf16[8192,512]{1,0:T(8,128)(2,1)}) %all-gather.3.cloned.1.call-update) | async-done | bytes 8388624 | tf_op jit(solution)/shard_map/all_gather | solution.py:88
  143.1 8.4 %fusion.9 = bf16[128,4096]{1,0:T(8,128)(2,1)} fusion(bf16[4096,512]{1,0:T(8,128)(2,1)} %all-gather.5.cloned.1.call-done, bf16[128,4096]{1,0:T(8,128)(2,1)} %param.14, bf16[128,8192]{1,0:T(8,128)(2,1)S(1)} %copy-done, bf16[8192,512]{1,0:T(8,128)(2,1)} %all-gather.3.cloned.1.call-done, s32[512]{0:T(512)S(1)} %add_select_fusion, s32[128]{0:T(128)} %param.18), kind=kOutput, calls=%fused_computation.28 | convolution fusion | flops 1612906496 | bytes 16779776 | tf_op jit(solution)/shard_map/dot_general | solution.py:92
  151.5 3.2 scatter_custom_fusion
  154.7 1.6 reshape.146
  156.3 3.9 %all-to-all-start = ((bf16[16,12,4096]{2,1,0:T(8,128)(2,1)}), bf16[16,12,4096]{2,1,0:T(8,128)(2,1)S(1)}, u32[]{:S(2)}, u32[]{:S(2)}) async-start(bf16[16,12,4096]{2,1,0:T(8,128)(2,1)} %reshape.146), calls=%async_computation | async-start | bytes 4194304 | tf_op jit(solution)/shard_map/all_to_all | solution.py:123
  164.1 3.3 gather_fusion
  167.3 3.2 gather_fusion.1
  172.8 28.2 %all-to-all-done = bf16[16,12,4096]{2,1,0:T(8,128)(2,1)S(1)} async-done(((bf16[16,12,4096]{2,1,0:T(8,128)(2,1)}), bf16[16,12,4096]{2,1,0:T(8,128)(2,1)S(1)}, u32[]{:S(2)}, u32[]{:S(2)}) %all-to-all-start) | async-done | bytes 1572896 | tf_op jit(solution)/shard_map/all_to_all | solution.py:123
  202.4 2.3 slice_bitcast_fusion.9
  204.7 2.0 reshape_reshape.6
  206.8 2.5 fusion.63
  211.0 6.0 %fusion.26 = f32[192,8,1536]{2,1,0:T(8,128)} fusion(bf16[192,8,128]{2,1,0:T(8,128)(2,1)S(1)} %bitcast.74, bf16[1536,512]{1,0:T(8,128)(2,1)} %bitcast.69), kind=kOutput, calls=%fused_computation.52 | convolution fusion | flops 603979776 | bytes 10223616 | tf_op jit(solution)/shard_map/rgd,ld->rgl/dot_general | solution.py:35
  217.0 1.4 fusion.25
  218.5 5.5 %fusion = (f32[192,8]{1,0:T(8,128)S(1)}, f32[192,8,1536]{2,1,0:T(8,128)}) fusion(pred[1536]{0:T(1024)(128)(4,1)S(1)} %iota_compare_fusion.2, bf16[192,8,128]{2,1,0:T(8,128)(2,1)S(1)} %bitcast.73, bf16[1536,512]{1,0:T(8,128)(2,1)S(1)} %bitcast.71), kind=kOutput, calls=%fused_computation.18 | convolution fusion | flops 611056128 | bytes 10231808 | tf_op jit(solution)/shard_map/rgd,ld->rgl/dot_general | solution.py:35
  224.0 13.8 %fusion.4 = (f32[192,8]{1,0:T(8,128)S(1)}, f32[192,8]{1,0:T(8,128)S(1)}, f32[192,8]{1,0:T(8,128)S(1)}, f32[192,8]{1,0:T(8,128)S(1)}, f32[192,8,1536]{2,1,0:T(8,128)}) fusion(f32[192,8,1536]{2,1,0:T(8,128)} %get-tuple-element.33, f32[192,8]{1,0:T(8,128)S(1)} %max.12, pred[1536]{0:T(1024)(128)(4,1)S(1)} %iota_compare_fusion.2, f32[192,8,1536]{2,1,0:T(8,128)} %fusion.26, ...), kind=kOutput, calls=%fused_computation.22 | convolution fusion | flops 634644480 | bytes 38660096 | tf_op jit(solution)/shard_map/rgd,ld->rgl/dot_general | solution.py:35
  237.8 5.1 %fusion.18 = bf16[192,8,128]{2,1,0:T(8,128)(2,1)S(1)} fusion(f32[192,8,1536]{2,1,0:T(8,128)} %get-tuple-element.33, f32[192,8]{1,0:T(8,128)S(1)} %get-tuple-element.17, f32[192,8]{1,0:T(8,128)S(1)} %max.12, pred[1536]{0:T(1024)(128)(4,1)S(1)} %iota_compare_fusion.2, bf16[1536,512]{1,0:T(8,128)(2,1)} %bitcast.76, f32[192,128]{1,0:T(8,128)S(1)} %copy-done.6, ...), kind=kOutput, calls=%fused_computation.38 | convolution fusion | flops 616366080 | bytes 10341888 | tf_op jit(solution)/shard_map/rgl,ld->rgd/dot_general | solution.py:46
  243.7 13.3 %fusion.5 = (f32[192,8]{1,0:T(8,128)S(1)}, f32[192,8]{1,0:T(8,128)S(1)}, f32[192,8]{1,0:T(8,128)S(1)}) fusion(f32[192,8,1536]{2,1,0:T(8,128)} %get-tuple-element.34, f32[192,8]{1,0:T(8,128)S(1)} %max.13, pred[1536]{0:T(1024)(128)(4,1)S(1)} %iota_compare_fusion.2, f32[192,8]{1,0:T(8,128)S(1)} %max.14, f32[192,8,1536]{2,1,0:T(8,128)} %fusion.26, ...), kind=kLoop, calls=%fused_computation.23 | loop fusion | flops 28306944 | bytes 28349952 | tf_op jit(solution)/shard_map/reduce_sum | solution.py:43
  257.8 3.2 fusion.19
  262.3 5.7 %fusion.20 = bf16[192,8,128]{2,1,0:T(8,128)(2,1)} fusion(f32[192,8,1536]{2,1,0:T(8,128)} %fusion.26, f32[192,8]{1,0:T(8,128)S(1)} %copy-done.7, f32[192,8]{1,0:T(8,128)S(1)} %max.14, pred[1536]{0:T(1024)(128)(4,1)S(1)} %iota_compare_fusion.2, bf16[1536,512]{1,0:T(8,128)(2,1)S(1)} %bitcast.78, f32[192,128]{1,0:T(8,128)S(1)} %get-tuple-element.26, ...), kind=kOutput, calls=%fused_computation.40 | convolution fusion | flops 616366080 | bytes 10526720 | tf_op jit(solution)/shard_map/rgl,ld->rgd/dot_general | solution.py:46
  268.0 2.1 convert_element_type.109
  270.1 5.0 %fusion.21 = bf16[192,8,128]{2,1,0:T(8,128)(2,1)S(1)} fusion(f32[192,8,1536]{2,1,0:T(8,128)} %copy-done.2, f32[192,8]{1,0:T(8,128)S(1)} %get-tuple-element.23, f32[192,8]{1,0:T(8,128)S(1)} %max.15, pred[1536]{0:T(1024)(128)(4,1)S(1)} %iota_compare_fusion.2, bf16[1536,512]{1,0:T(8,128)(2,1)S(1)} %bitcast.79, f32[192,128]{1,0:T(8,128)S(1)} %get-tuple-element.25, ...), kind=kOutput, calls=%fused_computation.41 | convolution fusion | flops 616366080 | bytes 10618880 | tf_op jit(solution)/shard_map/rgl,ld->rgd/dot_general | solution.py:46
  276.2 3.0 pad_maximum_fusion
  279.2 11.2 %all-to-all-start.3 = ((bf16[16,12,4096]{2,1,0:T(8,128)(2,1)}), bf16[16,12,4096]{2,1,0:T(8,128)(2,1)}, u32[]{:S(2)}, u32[]{:S(2)}) async-start(bf16[16,12,4096]{2,1,0:T(8,128)(2,1)} %pad_maximum_fusion), calls=%async_computation.3 | async-start | bytes 4194304 | tf_op jit(solution)/shard_map/all_to_all | solution.py:142
  290.4 41.1 %all-to-all-done.3 = bf16[16,12,4096]{2,1,0:T(8,128)(2,1)} async-done(((bf16[16,12,4096]{2,1,0:T(8,128)(2,1)}), bf16[16,12,4096]{2,1,0:T(8,128)(2,1)}, u32[]{:S(2)}, u32[]{:S(2)}) %all-to-all-start.3) | async-done | bytes 1572896 | tf_op jit(solution)/shard_map/all_to_all | solution.py:142
  331.6 3.6 %reshape.157 = bf16[192,4096]{1,0:T(8,128)(2,1)} reshape(bf16[16,12,4096]{2,1,0:T(8,128)(2,1)} %all-to-all-done.3) | data formatting | bytes 3145728 | tf_op jit(solution)/shard_map/reshape | solution.py:149
  335.1 4.8 %gather_fusion.2 = bf16[128,4096]{1,0:T(8,128)(2,1)} fusion(bf16[192,4096]{1,0:T(8,128)(2,1)} %reshape.157, s32[1024]{0:T(1024)S(1)} %pad_clamp_fusion), kind=kCustom, calls=%fused_computation.2 | custom fusion | bytes 2097664 | tf_op jit(solution)/shard_map/gather | solution.py:149
  (71 shorter events, 15.3 us)
Async XLA Ops:
  6.5 136.5 %copy-start = (bf16[128,8192]{1,0:T(8,128)(2,1)S(1)}, bf16[128,8192]{1,0:T(8,128)(2,1)}, u32[]{:S(2)}) copy-start(bf16[128,8192]{1,0:T(8,128)(2,1)} %param.13) | copy-start | bytes 6291460
  6.5 60.8 %all-gather.5.cloned.1.call-start = ((), (), s32[]{:S(2)}) async-start(), calls=%async_computation.5 | async-start | bytes 4456448 | tf_op jit(solution)/shard_map/all_gather | solution.py:94
  7.3 135.8 %all-gather.3.cloned.1.call-start = ((), (), s32[]{:S(2)}) async-start(), calls=%async_computation.4 | async-start | bytes 8912896 | tf_op jit(solution)/shard_map/all_gather | solution.py:88
  11.6 21.1 %all-to-all-start.1 = ((bf16[16,12,512]{2,1,0:T(8,128)(2,1)}), bf16[16,12,512]{2,1,0:T(8,128)(2,1)S(1)}, u32[]{:S(2)}, u32[]{:S(2)}) async-start(bf16[16,12,512]{2,1,0:T(8,128)(2,1)} %reshape.150), calls=%async_computation.1 | async-start | bytes 524288 | tf_op jit(solution)/shard_map/all_to_all | solution.py:124
  32.6 123.6 %all-to-all-start.2 = ((bf16[16,12,512]{2,1,0:T(8,128)(2,1)}), bf16[16,12,512]{2,1,0:T(8,128)(2,1)S(1)}, u32[]{:S(2)}, u32[]{:S(2)}) async-start(bf16[16,12,512]{2,1,0:T(8,128)(2,1)} %reshape.152), calls=%async_computation.2 | async-start | bytes 524288 | tf_op jit(solution)/shard_map/all_to_all | solution.py:127
  36.8 123.4 %copy-start.8 = (s32[16]{0:T(128)S(1)}, s32[16]{0:T(128)}, u32[]{:S(2)}) copy-start(s32[16]{0:T(128)} %param.19) | copy-start | bytes 196
  36.8 125.9 %copy-start.9 = (s32[16]{0:T(128)S(1)}, s32[16]{0:T(128)}, u32[]{:S(2)}) copy-start(s32[16]{0:T(128)} %param.21) | copy-start | bytes 196
  156.3 44.8 %all-to-all-start = ((bf16[16,12,4096]{2,1,0:T(8,128)(2,1)}), bf16[16,12,4096]{2,1,0:T(8,128)(2,1)S(1)}, u32[]{:S(2)}, u32[]{:S(2)}) async-start(bf16[16,12,4096]{2,1,0:T(8,128)(2,1)} %reshape.146), calls=%async_computation | async-start | bytes 4194304 | tf_op jit(solution)/shard_map/all_to_all | solution.py:123
  206.8 10.2 %copy-start.3 = (bf16[12,128,512]{2,1,0:T(8,128)(2,1)S(1)}, bf16[12,128,512]{2,1,0:T(8,128)(2,1)}, u32[]{:S(2)}) copy-start(bf16[12,128,512]{2,1,0:T(8,128)(2,1)} %gather_fusion) | copy-start | bytes 4718596
  218.4 19.4 %copy-start.2 = (f32[192,8,1536]{2,1,0:T(8,128)}, f32[192,8,1536]{2,1,0:T(8,128)S(1)}, u32[]{:S(2)}) copy-start(f32[192,8,1536]{2,1,0:T(8,128)S(1)} %fusion.25) | copy-start | bytes 28311556
  224.0 13.8 %copy-start.6 = (f32[192,128]{1,0:T(8,128)S(1)}, f32[192,128]{1,0:T(8,128)}, u32[]{:S(2)}) copy-start(f32[192,128]{1,0:T(8,128)} %get-tuple-element.24) | copy-start | bytes 294916
  243.6 14.2 %slice-start = ((s8[9437184]{0:T(1024)(128)(4,1)}), s8[4194304]{0:T(1024)(128)(4,1)S(1)}, s32[]{:S(2)}) async-start(s8[9437184]{0:T(1024)(128)(4,1)} %bitcast.67), calls=%async_computation.6 | async-start | bytes 8388608
  243.7 14.1 %slice-start.1 = ((s8[9437184]{0:T(1024)(128)(4,1)}), s8[4194304]{0:T(1024)(128)(4,1)S(1)}, s32[]{:S(2)}) async-start(s8[9437184]{0:T(1024)(128)(4,1)} %bitcast.67), calls=%async_computation.7 | async-start | bytes 8388608
  243.7 14.1 %slice-start.2 = ((s8[9437184]{0:T(1024)(128)(4,1)}), s8[1048576]{0:T(1024)(128)(4,1)S(1)}, s32[]{:S(2)}) async-start(s8[9437184]{0:T(1024)(128)(4,1)} %bitcast.67), calls=%async_computation.8 | async-start | bytes 2097152
  243.7 14.1 %copy-start.4 = (bf16[12,128,512]{2,1,0:T(8,128)(2,1)S(1)}, bf16[12,128,512]{2,1,0:T(8,128)(2,1)}, u32[]{:S(2)}) copy-start(bf16[12,128,512]{2,1,0:T(8,128)(2,1)} %gather_fusion.1) | copy-start | bytes 4718596
  243.7 14.1 %copy-start.5 = (f32[192,128]{1,0:T(8,128)S(1)}, f32[192,128]{1,0:T(8,128)}, u32[]{:S(2)}) copy-start(f32[192,128]{1,0:T(8,128)} %get-tuple-element.27) | copy-start | bytes 294916
  257.8 4.5 %copy-start.7 = (f32[192,8]{1,0:T(8,128)S(1)}, f32[192,8]{1,0:T(8,128)}, u32[]{:S(2)}) copy-start(f32[192,8]{1,0:T(8,128)} %get-tuple-element.35) | copy-start | bytes 18436
  276.2 63.7 %copy-start.1 = (bf16[128,8192]{1,0:T(8,128)(2,1)S(1)}, bf16[128,8192]{1,0:T(8,128)(2,1)}, u32[]{:S(2)}) copy-start(bf16[128,8192]{1,0:T(8,128)(2,1)} %param.13) | copy-start | bytes 6291460
  279.2 52.4 %all-to-all-start.3 = ((bf16[16,12,4096]{2,1,0:T(8,128)(2,1)}), bf16[16,12,4096]{2,1,0:T(8,128)(2,1)}, u32[]{:S(2)}, u32[]{:S(2)}) async-start(bf16[16,12,4096]{2,1,0:T(8,128)(2,1)} %pad_maximum_fusion), calls=%async_computation.3 | async-start | bytes 4194304 | tf_op jit(solution)/shard_map/all_to_all | solution.py:142
Sparse Core Ops, SparseCore 0:
  9.5 57.7 all-gather.4
  69.5 73.5 all-gather.2
where the time goes:
time: 353 us; the launch traced here: 347 us
  waiting for transfers between devices  188 us (53%)
  matrix products  56.7 us (16%)
  local copies, waits for them, and re-layouts  38 us (11%)
  starting transfers between devices  26.7 us (8%)
  other arithmetic  21.1 us (6%)
  between operations  15.8 us (4%)
    all_gather x1, waiting for transfers between devices, on_device(): lax.all_gather(adapter_down_weight, 'score', axis=0, tiled=True)  75.7 us
    all_to_all x1, waiting for transfers between devices, on_device(): lax.all_to_all(answer.reshape(array_shape[0], array_shape[1], width), 'sc...  41.1 us
    all_gather x1, waiting for transfers between devices, on_device(): lax.all_gather(adapter_up_weight, 'score', axis=0, tiled=True)  30.5 us
    all_to_all x1, waiting for transfers between devices, on_device(): lax.all_to_all(place(query), 'score', split_axis=0, concat_axis=0, tiled=...  28.2 us
    dot_general x4, matrix products, attend_core(): jnp.einsum('rgd,ld->rgl', head_list, key_head, preferred_element_type=jnp...  26.7 us
    dot_general x4, matrix products, attend_core(): jnp.einsum('rgl,ld->rgd', weights, value_head, preferred_element_type=jnp...  19 us
    reduce_sum x1, other arithmetic, attend_core(): total = jnp.sum(weights, -1) + self_weight  13.3 us
    all_to_all x1, waiting for transfers between devices, on_device(): lax.all_to_all(place(answer_row_key), 'score', split_axis=0, concat_axis=...  11.4 us
  transfers between devices with their start and end apart: 6, of which 5 were waited for; matrix products, arithmetic and copies ran while one was open for 9% of the time, Pallas kernels for 0%

commit v1 on v0

v1 whole, which is shorter than its diff:
```python
import functools

import jax
import jax.numpy as jnp
from jax import lax
from jax.experimental import pallas as pl
from jax.experimental.pallas import tpu as pltpu
from jax.sharding import PartitionSpec as P

QUERY_HEADS = 32
KEY_VALUE_HEADS = 4
HEAD_GROUP = QUERY_HEADS // KEY_VALUE_HEADS
HEAD_SIZE = 128
ADAPTER_RANK = 64
BLOCK_TOKENS = 128
MAXB = 12
TOKEN_SPAN = MAXB * BLOCK_TOKENS
SCORE_SCALE = 1.4426950408889634 / HEAD_SIZE**0.5
CHUNK = 256


def attend_kernel(
    frozen_ref, masked_ref, up_ref, key_ref, value_ref, self_key_ref, self_value_ref, bias_ref,
    out_ref, change_ref,
):
    slots = masked_ref.shape[0]
    for head in range(HEAD_GROUP):
        change_ref[pl.ds(head, slots, stride=HEAD_GROUP), :] = lax.dot_general(
            masked_ref[...],
            up_ref[head * HEAD_SIZE : (head + 1) * HEAD_SIZE, :],
            (((1,), (1,)), ((), ())),
            preferred_element_type=jnp.float32,
        )
    keys = key_ref[...].reshape(TOKEN_SPAN, HEAD_SIZE)
    values = value_ref[...].reshape(TOKEN_SPAN, HEAD_SIZE)
    bias = bias_ref[...]

    def spread(rows):
        wide = rows.astype(jnp.float32)[:, None, :]
        return jnp.broadcast_to(wide, (rows.shape[0], HEAD_GROUP, HEAD_SIZE)).reshape(
            rows.shape[0] * HEAD_GROUP, HEAD_SIZE
        )

    for start in range(0, slots * HEAD_GROUP, CHUNK):
        part = slice(start, start + CHUNK)
        part_slots = slice(start // HEAD_GROUP, (start + CHUNK) // HEAD_GROUP)
        query = (frozen_ref[part, :].astype(jnp.float32) + 2.0 * change_ref[part, :]).astype(
            jnp.bfloat16
        )
        scores = (
            lax.dot_general(
                query, keys, (((1,), (1,)), ((), ())), preferred_element_type=jnp.float32
            )
            * SCORE_SCALE
            + bias
        )
        own = (
            jnp.sum(
                query.astype(jnp.float32) * spread(self_key_ref[part_slots, :]), 1, keepdims=True
            )
            * SCORE_SCALE
        )
        top = jnp.maximum(jnp.max(scores, 1, keepdims=True), own)
        weights = jnp.exp2(scores - top)
        self_weight = jnp.exp2(own - top)
        inverse = 1.0 / (jnp.sum(weights, 1, keepdims=True) + self_weight)
        mixed = jnp.dot(
            (weights * inverse).astype(jnp.bfloat16), values, preferred_element_type=jnp.float32
        )
        self_weight = (self_weight * inverse).astype(jnp.bfloat16).astype(jnp.float32)
        out_ref[part, :] = (mixed + self_weight * spread(self_value_ref[part_slots, :])).astype(
            jnp.bfloat16
        )


def attend(frozen, masked, up, keys, values, self_rows, bias):
    slots, columns = masked.shape
    items = slots * HEAD_GROUP
    head_blocks = (MAXB, BLOCK_TOKENS, HEAD_SIZE)
    return pl.pallas_call(
        attend_kernel,
        grid=(KEY_VALUE_HEADS,),
        in_specs=[
            pl.BlockSpec((items, HEAD_SIZE), lambda g: (0, g)),
            pl.BlockSpec((slots, columns), lambda g: (0, 0)),
            pl.BlockSpec((HEAD_GROUP * HEAD_SIZE, columns), lambda g: (g, 0)),
            pl.BlockSpec(head_blocks, lambda g: (0, 0, g)),
            pl.BlockSpec(head_blocks, lambda g: (0, 0, g)),
            pl.BlockSpec((slots, HEAD_SIZE), lambda g: (0, g)),
            pl.BlockSpec((slots, HEAD_SIZE), lambda g: (0, KEY_VALUE_HEADS + g)),
            pl.BlockSpec((1, TOKEN_SPAN), lambda g: (0, 0)),
        ],
        out_specs=pl.BlockSpec((items, HEAD_SIZE), lambda g: (0, g)),
        out_shape=jax.ShapeDtypeStruct((items, KEY_VALUE_HEADS * HEAD_SIZE), jnp.bfloat16),
        scratch_shapes=[pltpu.VMEM((items, HEAD_SIZE), jnp.float32)],
        compiler_params=pltpu.CompilerParams(vmem_limit_bytes=48 * 1024 * 1024),
        name="attend",
    )(frozen, masked, up, keys, values, self_rows, self_rows, bias)


def on_device(
    hidden,
    frozen_query_rows,
    answer_row_key,
    answer_row_value,
    row_request_index,
    row_checkpoint_index,
    request_device_owner,
    request_block_table,
    request_prefix_length,
    adapter_down_weight,
    adapter_up_weight,
    paged_key_blocks,
    paged_value_blocks,
):
    rows = hidden.shape[0]
    devices = lax.axis_size("score")
    capacity = max(2, (3 * rows + 2 * devices - 1) // (2 * devices))
    slots = devices * capacity
    width = frozen_query_rows.shape[1]
    kv_width = answer_row_key.shape[1]
    column_list = adapter_down_weight.shape[1]

    req_ids = jnp.arange(devices, dtype=jnp.int32)
    requests = row_request_index[:, 0]
    picked = requests[:, None] == req_ids[None, :]
    target = jnp.sum(jnp.where(picked, request_device_owner[None, :], 0), 1)
    hits = (target[:, None] == req_ids[None, :]).astype(jnp.int32)
    before = jnp.cumsum(hits, 0) - hits
    slot = target * capacity + jnp.sum(before * hits, 1)
    chooser = (jnp.arange(slots, dtype=jnp.int32)[:, None] == slot[None, :]).astype(jnp.bfloat16)

    def place(value_rows):
        return jnp.dot(chooser, value_rows, preferred_element_type=jnp.float32).astype(
            jnp.bfloat16
        )

    def exchange(filled):
        parts = filled.reshape(devices, filled.shape[0] // devices, filled.shape[1])
        moved = lax.all_to_all(parts, "score", split_axis=0, concat_axis=0, tiled=True)
        return moved.reshape(filled.shape)

    frozen = (
        place(frozen_query_rows)
        .reshape(slots, KEY_VALUE_HEADS, HEAD_GROUP, HEAD_SIZE)
        .transpose(0, 2, 1, 3)
        .reshape(slots * HEAD_GROUP, kv_width)
    )
    frozen = exchange(frozen)
    self_rows = exchange(place(jnp.concatenate([answer_row_key, answer_row_value], 1)))

    down = lax.all_gather(adapter_down_weight, "score", axis=0, tiled=True)
    up = lax.all_gather(adapter_up_weight, "score", axis=0, tiled=True)
    column_owner = jnp.arange(column_list, dtype=jnp.int32) // ADAPTER_RANK
    chosen = row_checkpoint_index[:, None] == column_owner[None, :]
    inner = jnp.dot(hidden, down, preferred_element_type=jnp.float32)
    masked = exchange(place(jnp.where(chosen, inner, 0.0).astype(jnp.bfloat16)))

    here = lax.axis_index("score")
    local_req = jnp.sum(jnp.where(request_device_owner == here, req_ids, 0))
    order = lax.dynamic_index_in_dim(request_block_table, local_req, 0, keepdims=False)
    length = lax.dynamic_index_in_dim(request_prefix_length, local_req, 0, keepdims=False)
    blocks = jnp.arange(MAXB, dtype=jnp.int32)
    place_of = jnp.sum(jnp.where(order[None, :] == blocks[:, None], blocks[None, :], 0), 1)
    position = place_of[:, None] * BLOCK_TOKENS + jnp.arange(BLOCK_TOKENS, dtype=jnp.int32)[None, :]
    bias = jnp.where(position < length, 0.0, -jnp.inf).astype(jnp.float32).reshape(1, TOKEN_SPAN)

    answer = attend(frozen, masked, up, paged_key_blocks, paged_value_blocks, self_rows, bias)
    returned = exchange(answer).reshape(slots, HEAD_GROUP, kv_width)[slot]
    return (
        returned.reshape(rows, HEAD_GROUP, KEY_VALUE_HEADS, HEAD_SIZE)
        .transpose(0, 2, 1, 3)
        .reshape(rows, width)
    )


def solution(mesh):
    placed = (
        P(("groups", "score"), None),
        P(("groups", "score"), None),
        P(("groups", "score"), None),
        P(("groups", "score"), None),
        P(("groups", "score"), None),
        P(("groups", "score")),
        P("groups"),
        P("groups", None),
        P("groups"),
        P("score", None),
        P("score", None),
        P(("groups", "score"), None, None),
        P(("groups", "score"), None, None),
    )
    return jax.shard_map(
        on_device,
        mesh=mesh,
        in_specs=placed,
        out_specs=P(("groups", "score"), None),
        check_vma=False,
    )
```

time: 353 us -> 257 us (0.73)
  matrix products: 56.7 us -> 7.82 us
  local copies, waits for them, and re-layouts: 38 us -> 10.6 us
  Pallas kernels: 0 us -> 25.2 us
  waiting for transfers between devices: 188 us -> 166 us
  other arithmetic: 21.1 us -> 2.77 us
    dot_general x10 -> x3, matrix products: 56.7 us -> 7.82 us  [place(): jnp.dot(chooser, value_rows, preferred_element_type=jnp.float32)]
    all_gather x2, waiting for transfers between devices: 106 us -> 77.8 us  [the longest x1 77.8 us: on_device(): down = lax.all_gather(adapter_down_weight, 'score', axis=0, tiled=True)]
    pallas_call x0 -> x1, Pallas kernels: none -> 25.2 us  [attend(): pl.pallas_call(attend_kernel, grid=(KEY_VALUE_HEADS,), in_specs=[pl.Block...]
    reduce_sum x2, other arithmetic: 13.5 us -> 0.29 us  [the longest x1 0.17 us: on_device(): slot = target * capacity + jnp.sum(before * hits, 1)]
    gather x3 -> x1, local copies, waits for them, and re-layouts: 11.3 us -> 2.05 us  [on_device(): returned = exchange(answer).reshape(slots, HEAD_GROUP, kv_width)[slot]]
    reshape x6 -> x4, local copies, waits for them, and re-layouts: 8 us -> 1.77 us  [the longest x2 1.63 us: exchange(): parts = filled.reshape(devices, filled.shape[0] // devices, filled.shape[1])]
    scatter x3 -> x0, local copies, waits for them, and re-layouts: 6.17 us -> none  [place(): filled = jnp.zeros((devices * capacity, value_rows.shape[1]), value_rows....]
    all_to_all x4, waiting for transfers between devices: 80.8 us -> 86.9 us  [exchange(): lax.all_to_all(parts, 'score', split_axis=0, concat_axis=0, tiled=True)]
  transfers between devices with their start and end apart: 6 -> 6, of which waited for: 5 -> 5; matrix products, arithmetic and copies ran while one was open for 9% -> 6% of each run, Pallas kernels for 0% -> 0%
where the time goes in v1:
time: 257 us; the launch traced here: 252 us
  waiting for transfers between devices  166 us (65%)
  Pallas kernels  25.2 us (10%)
  starting transfers between devices  24.4 us (9%)
  between operations  15.5 us (6%)
  local copies, waits for them, and re-layouts  10.6 us (4%)
  matrix products  7.82 us (3%)
  other arithmetic  2.77 us (1%)
    all_to_all x4, waiting for transfers between devices, exchange(): lax.all_to_all(parts, 'score', split_axis=0, concat_axis=0, tiled=True)  86.9 us
    all_gather x1, waiting for transfers between devices, on_device(): down = lax.all_gather(adapter_down_weight, 'score', axis=0, tiled=True)  77.8 us
    pallas_call x1, Pallas kernels, attend(): pl.pallas_call(attend_kernel, grid=(KEY_VALUE_HEADS,), in_specs=[pl.Block...  25.2 us
    all_to_all x4, starting transfers between devices, exchange(): lax.all_to_all(parts, 'score', split_axis=0, concat_axis=0, tiled=True)  24.3 us
    dot_general x3, matrix products, place(): jnp.dot(chooser, value_rows, preferred_element_type=jnp.float32)  7.82 us
    unnamed x15, local copies, waits for them, and re-layouts  5.51 us
  transfers between devices with their start and end apart: 6, of which 5 were waited for; matrix products, arithmetic and copies ran while one was open for 6% of the time, Pallas kernels for 0%

profile of v1, /device:TPU:0, one launch (start us, length us, event | category | flops | bytes accessed | tf_op | source)
XLA Modules:
  0.0 252.3 jit_solution(349562128038715778)
XLA Ops:
  6.5 0.7 all-gather.3.cloned.1.call-update
  7.3 0.7 all-gather.5.cloned.1.call-update
  8.0 0.8 select_reduce_fusion.1
  8.9 0.1 fusion.9
  9.0 0.2 reduce_window_sum.11
  9.1 0.2 select_reduce_fusion
  9.3 1.2 convolution_convert_fusion.1
  10.5 0.9 reshape.117
  11.4 7.4 %all-to-all-start.2 = ((bf16[16,12,1024]{2,1,0:T(8,128)(2,1)}), bf16[16,12,1024]{2,1,0:T(8,128)(2,1)S(1)}, u32[]{:S(2)}, u32[]{:S(2)}) async-start(bf16[16,12,1024]{2,1,0:T(8,128)(2,1)} %reshape.117), calls=%async_computation.2 | async-start | bytes 1048576 | tf_op jit(solution)/shard_map/all_to_all | solution.py:140
  18.8 77.8 %all-gather.3.cloned.1.call-done = bf16[8192,512]{1,0:T(8,128)(2,1)} async-done(((bf16[512,512]{1,0:T(8,128)(2,1)}), bf16[8192,512]{1,0:T(8,128)(2,1)}) %all-gather.3.cloned.1.call-update) | async-done | bytes 8388624 | tf_op jit(solution)/shard_map/all_gather | solution.py:152
  96.6 4.8 %convolution_convert_fusion.2 = bf16[192,512]{1,0:T(8,128)(2,1)S(1)} fusion(bf16[128,8192]{1,0:T(8,128)(2,1)S(1)} %copy-done, bf16[8192,512]{1,0:T(8,128)(2,1)} %all-gather.3.cloned.1.call-done, s32[512]{0:T(512)S(1)} %add_select_fusion, s32[128]{0:T(128)S(1)} %copy-done.3, s32[128]{0:T(128)S(1)} %get-tuple-element.6), kind=kOutput, calls=%fused_computation.4 | convolution fusion | flops 1099227136 | bytes 10685440 | tf_op jit(solution)/shard_map/dot_general | solution.py:134
  101.4 0.7 reshape.115
  102.2 3.5 %all-to-all-start.1 = ((bf16[16,12,512]{2,1,0:T(8,128)(2,1)}), bf16[16,12,512]{2,1,0:T(8,128)(2,1)S(1)}, u32[]{:S(2)}, u32[]{:S(2)}) async-start(bf16[16,12,512]{2,1,0:T(8,128)(2,1)} %reshape.115), calls=%async_computation.1 | async-start | bytes 524288 | tf_op jit(solution)/shard_map/all_to_all | solution.py:140
  105.7 1.8 fusion
  107.5 1.5 copy.14
  109.0 11.0 %all-to-all-done.1 = bf16[16,12,512]{2,1,0:T(8,128)(2,1)S(1)} async-done(((bf16[16,12,512]{2,1,0:T(8,128)(2,1)}), bf16[16,12,512]{2,1,0:T(8,128)(2,1)S(1)}, u32[]{:S(2)}, u32[]{:S(2)}) %all-to-all-start.1) | async-done | bytes 196640 | tf_op jit(solution)/shard_map/all_to_all | solution.py:140
  120.0 4.4 %all-to-all-start = ((bf16[16,96,512]{2,1,0:T(8,128)(2,1)}), bf16[16,96,512]{2,1,0:T(8,128)(2,1)}, u32[]{:S(2)}, u32[]{:S(2)}) async-start(bf16[16,96,512]{2,1,0:T(8,128)(2,1)} %bitcast.38), calls=%async_computation | async-start | bytes 3145728 | tf_op jit(solution)/shard_map/all_to_all | solution.py:140
  124.4 0.6 fusion.16
  127.0 0.6 dynamic_slice.9
  127.6 0.7 dynamic-slice_bitcast_fusion
  128.3 0.1 select_reduce_fusion.2
  128.4 0.7 select_bitcast_fusion
  129.1 0.1 reshape.118.self_key_ref.self_value_ref
  129.3 43.9 %all-to-all-done = bf16[16,96,512]{2,1,0:T(8,128)(2,1)} async-done(((bf16[16,96,512]{2,1,0:T(8,128)(2,1)}), bf16[16,96,512]{2,1,0:T(8,128)(2,1)}, u32[]{:S(2)}, u32[]{:S(2)}) %all-to-all-start) | async-done | bytes 1572896 | tf_op jit(solution)/shard_map/all_to_all | solution.py:140
  173.2 0.1 all-gather.5.cloned.1.call-done.up_ref
  173.2 1.4 copy-done.2
  174.6 25.2 %attend.1 = bf16[1536,512]{1,0:T(8,128)(2,1)S(1)} custom-call(bf16[1536,512]{1,0:T(8,128)(2,1)} %bitcast.3.frozen_ref, bf16[192,512]{1,0:T(8,128)(2,1)S(1)} %reshape.116.masked_ref, bf16[4096,512]{1,0:T(8,128)(2,1)} %all-gather.5.cloned.1.call-done.up_ref, bf16[12,128,512]{2,1,0:T(8,128)(2,1)S(1)} %copy-done.2, bf16[12,128,512]{2,1,0:T(8,128)(2,1)} %value_ref.1, ...), custom_call_target="tpu_custom_call" | custom-call | tf_op jit(solution)/shard_map/attend/pallas_call | solution.py:80
  199.8 1.2 copy-done.1
  201.0 9.0 %all-to-all-start.3 = ((bf16[16,96,512]{2,1,0:T(8,128)(2,1)}), bf16[16,96,512]{2,1,0:T(8,128)(2,1)}, u32[]{:S(2)}, u32[]{:S(2)}) async-start(bf16[16,96,512]{2,1,0:T(8,128)(2,1)} %bitcast.36), calls=%async_computation.3 | async-start | bytes 3145728 | tf_op jit(solution)/shard_map/all_to_all | solution.py:140
  210.0 32.0 %all-to-all-done.3 = bf16[16,96,512]{2,1,0:T(8,128)(2,1)} async-done(((bf16[16,96,512]{2,1,0:T(8,128)(2,1)}), bf16[16,96,512]{2,1,0:T(8,128)(2,1)}, u32[]{:S(2)}, u32[]{:S(2)}) %all-to-all-start.3) | async-done | bytes 1572896 | tf_op jit(solution)/shard_map/all_to_all | solution.py:140
  242.0 2.1 gather_fusion
  244.1 1.4 copy.19
  (19 shorter events, 0.1 us)
Async XLA Ops:
  6.5 90.1 %copy-start = (bf16[128,8192]{1,0:T(8,128)(2,1)S(1)}, bf16[128,8192]{1,0:T(8,128)(2,1)}, u32[]{:S(2)}) copy-start(bf16[128,8192]{1,0:T(8,128)(2,1)} %param.13) | copy-start | bytes 6291460
  6.5 90.1 %copy-start.3 = (s32[128]{0:T(128)S(1)}, s32[128]{0:T(128)}, u32[]{:S(2)}) copy-start(s32[128]{0:T(128)} %param.18) | copy-start | bytes 1540
  6.5 90.0 %all-gather.3.cloned.1.call-start = ((), (), s32[]{:S(2)}) async-start(), calls=%async_computation.4 | async-start | bytes 8912896 | tf_op jit(solution)/shard_map/all_gather | solution.py:152
  7.3 166.0 %all-gather.5.cloned.1.call-start = ((), (), s32[]{:S(2)}) async-start(), calls=%async_computation.5 | async-start | bytes 4456448 | tf_op jit(solution)/shard_map/all_gather | solution.py:153
  11.4 90.7 %all-to-all-start.2 = ((bf16[16,12,1024]{2,1,0:T(8,128)(2,1)}), bf16[16,12,1024]{2,1,0:T(8,128)(2,1)S(1)}, u32[]{:S(2)}, u32[]{:S(2)}) async-start(bf16[16,12,1024]{2,1,0:T(8,128)(2,1)} %reshape.117), calls=%async_computation.2 | async-start | bytes 1048576 | tf_op jit(solution)/shard_map/all_to_all | solution.py:140
  102.2 17.8 %all-to-all-start.1 = ((bf16[16,12,512]{2,1,0:T(8,128)(2,1)}), bf16[16,12,512]{2,1,0:T(8,128)(2,1)S(1)}, u32[]{:S(2)}, u32[]{:S(2)}) async-start(bf16[16,12,512]{2,1,0:T(8,128)(2,1)} %reshape.115), calls=%async_computation.1 | async-start | bytes 524288 | tf_op jit(solution)/shard_map/all_to_all | solution.py:140
  109.0 15.4 %copy-start.4 = (s32[16]{0:T(128)S(1)}, s32[16]{0:T(128)}, u32[]{:S(2)}) copy-start(s32[16]{0:T(128)} %param.19) | copy-start | bytes 196
  109.0 18.0 %copy-start.5 = (s32[16]{0:T(128)S(1)}, s32[16]{0:T(128)}, u32[]{:S(2)}) copy-start(s32[16]{0:T(128)} %param.21) | copy-start | bytes 196
  120.0 53.2 %all-to-all-start = ((bf16[16,96,512]{2,1,0:T(8,128)(2,1)}), bf16[16,96,512]{2,1,0:T(8,128)(2,1)}, u32[]{:S(2)}, u32[]{:S(2)}) async-start(bf16[16,96,512]{2,1,0:T(8,128)(2,1)} %bitcast.38), calls=%async_computation | async-start | bytes 3145728 | tf_op jit(solution)/shard_map/all_to_all | solution.py:140
  173.2 1.4 copy-start.2
  199.8 1.2 copy-start.1
  201.0 41.1 %all-to-all-start.3 = ((bf16[16,96,512]{2,1,0:T(8,128)(2,1)}), bf16[16,96,512]{2,1,0:T(8,128)(2,1)}, u32[]{:S(2)}, u32[]{:S(2)}) async-start(bf16[16,96,512]{2,1,0:T(8,128)(2,1)} %bitcast.36), calls=%async_computation.3 | async-start | bytes 3145728 | tf_op jit(solution)/shard_map/all_to_all | solution.py:140
Sparse Core Ops, SparseCore 0:
  9.5 87.0 all-gather.2
  98.7 74.4 all-gather.4

commit v2 on v1

--- a/solution.py
+++ b/solution.py
@@ -98,6 +98,236 @@
     )(frozen, masked, up, keys, values, self_rows, self_rows, bias)
 
 
+def ring_chip(place, chips):
+    half = chips // 2
+    side = lax.div(place, half)
+    step = lax.rem(place, half)
+    return 2 * (step * (1 - side) + (half - 1 - step) * side) + side
+
+
+def feed_kernel(
+    devices, hidden_ref, chosen_ref, chooser_ref, down_ref, up_ref, frozen_ref, self_ref,
+    up_full, frozen_out, self_out, masked_out,
+    down_full, total, masked_send, pieces, row_sems, local_sems,
+):
+    chips = devices // 2
+    group = lax.axis_index("groups")
+    here = lax.axis_index("score")
+    chip, core = lax.div(here, 2), lax.rem(here, 2)
+    step_of, side = lax.div(chip, 2), lax.rem(chip, 2)
+    place = side * (chips - 1 - step_of) + (1 - side) * step_of
+    after = ring_chip(lax.rem(place + 1, chips), chips) * 2 + core
+    before = ring_chip(lax.rem(place + chips - 1, chips), chips) * 2 + core
+    sibling = chip * 2 + 1 - core
+    next_on = (after, before)
+    sources = (down_ref, up_ref)
+    fulls = (down_full, up_full)
+    parts = HEAD_SIZE
+
+    barrier = pltpu.get_barrier_semaphore()
+
+    @pl.loop(1, devices)
+    def _(offset):
+        pl.semaphore_signal(
+            barrier, inc=1, device_id={"score": lax.rem(here + offset, devices)},
+            device_id_type=pl.DeviceIdType.MESH,
+        )
+
+    pl.semaphore_signal(
+        barrier, inc=1, device_id={"groups": 1 - group}, device_id_type=pl.DeviceIdType.MESH
+    )
+    pl.semaphore_wait(barrier, devices)
+
+    def remote(source, target, send, recv, device):
+        return pltpu.make_async_remote_copy(
+            src_ref=source, dst_ref=target, send_sem=send, recv_sem=recv, device_id=device,
+            device_id_type=pl.DeviceIdType.MESH,
+        )
+
+    def shard(a, owner, quarter=None):
+        rows = sources[a].shape[0]
+        span = pl.ds(pl.multiple_of(owner * rows, rows), rows)
+        if quarter is None:
+            return fulls[a].at[span, :]
+        return fulls[a].at[span, pl.ds(pl.multiple_of(quarter * parts, parts), parts)]
+
+    def origin(d, t):
+        turn = place + chips - t if d == 0 else place + t
+        return ring_chip(lax.rem(turn, chips), chips)
+
+    def ring(a, d, t):
+        ref = shard(a, origin(d, t) * 2 + core, group * 2 + d)
+        return remote(ref, ref, pieces.at[0, a, d, t], pieces.at[1, a, d, t], {"score": next_on[d]})
+
+    def beside(a, d, t):
+        ref = shard(a, origin(d, t) * 2 + core, group * 2 + d)
+        return remote(ref, ref, pieces.at[2, a, d, t], pieces.at[3, a, d, t], {"score": sibling})
+
+    def across(a, d, t):
+        ref = shard(a, origin(d, t) * 2 + core, group * 2 + d)
+        return remote(ref, ref, pieces.at[4, a, d, t], pieces.at[5, a, d, t], {"groups": 1 - group})
+
+    def onward(a, d, t):
+        ref = shard(a, origin(d, t) * 2 + core, (1 - group) * 2 + d)
+        return remote(ref, ref, pieces.at[6, a, d, t], pieces.at[7, a, d, t], {"score": sibling})
+
+    def whole(a):
+        ref = shard(a, here)
+        return remote(ref, ref, pieces.at[2, a, 0, 0], pieces.at[3, a, 0, 0], {"score": sibling})
+
+    def rows_to(kind, offset):
+        peer = lax.rem(here + offset, devices)
+        source = (frozen_ref, self_ref, masked_send)[kind]
+        target = (frozen_out, self_out, masked_out)[kind]
+        size = source.shape[0] // devices
+        return remote(
+            source.at[pl.ds(pl.multiple_of(peer * size, size), size), :],
+            target.at[pl.ds(pl.multiple_of(here * size, size), size), :],
+            row_sems.at[0, kind, offset],
+            row_sems.at[1, kind, offset],
+            {"score": peer},
+        )
+
+    def rows_here(kind):
+        source = (frozen_ref, self_ref, masked_send)[kind]
+        target = (frozen_out, self_out, masked_out)[kind]
+        size = source.shape[0] // devices
+        span = pl.ds(pl.multiple_of(here * size, size), size)
+        return pltpu.make_async_copy(source.at[span, :], target.at[span, :], local_sems.at[2 + kind])
+
+    own = [pltpu.make_async_copy(sources[a], shard(a, here), local_sems.at[a]) for a in range(2)]
+    for copy in own:
+        copy.start()
+    rows_here(0).start()
+    rows_here(1).start()
+    for copy in own:
+        copy.wait()
+
+    def begin(a):
+        for d in range(2):
+            ring(a, d, 0).start()
+        whole(a).start()
+
+    def circle(a):
+        @pl.loop(0, chips - 1)
+        def _(t):
+            for d in range(2):
+                ring(a, d, t).wait_recv()
+
+                @pl.when(t < chips - 2)
+                def _():
+                    ring(a, d, t + 1).start()
+
+                across(a, d, t + 1).start()
+                beside(a, d, t + 1).start()
+            if a == 0:
+                for extra in range(2):
+                    rows_to(0, 2 * t + 1 + extra).start()
+                    rows_to(1, 2 * t + 1 + extra).start()
+
+            @pl.when(t > 0)
+            def _():
+                for d in range(2):
+                    across(a, d, t).wait_recv()
+                    onward(a, d, t).start()
+
+    def finish(a):
+        for d in range(2):
+            across(a, d, chips - 1).wait_recv()
+            onward(a, d, chips - 1).start()
+        whole(a).wait_recv()
+
+        @pl.loop(1, chips)
+        def _(t):
+            for d in range(2):
+                beside(a, d, t).wait_recv()
+                onward(a, d, t).wait_recv()
+
+    begin(0)
+    rows_to(0, devices - 1).start()
+    rows_to(1, devices - 1).start()
+    circle(0)
+    begin(1)
+    finish(0)
+
+    total[...] = jnp.zeros_like(total)
+    depth = hidden_ref.shape[1] // 8
+
+    @pl.loop(0, 8)
+    def _(k):
+        span = pl.ds(pl.multiple_of(k * depth, depth), depth)
+        total[...] += jnp.dot(
+            hidden_ref[:, span], down_full[span, :], preferred_element_type=jnp.float32
+        )
+
+    masked = jnp.where(chosen_ref[...] != 0, total[...], 0.0).astype(jnp.bfloat16)
+    masked_send[...] = jnp.dot(
+        chooser_ref[...], masked, preferred_element_type=jnp.float32
+    ).astype(jnp.bfloat16)
+    rows_here(2).start()
+
+    @pl.loop(1, devices)
+    def _(offset):
+        rows_to(2, offset).start()
+
+    circle(1)
+    finish(1)
+
+    for kind in range(3):
+        rows_here(kind).wait()
+
+    @pl.loop(1, devices)
+    def _(offset):
+        for kind in range(3):
+            rows_to(kind, offset).wait()
+
+    for a in range(2):
+        whole(a).wait_send()
+        for d in range(2):
+            ring(a, d, 0).wait_send()
+
+        @pl.loop(1, chips)
+        def _(t):
+            for d in range(2):
+                @pl.when(t < chips - 1)
+                def _():
+                    ring(a, d, t).wait_send()
+
+                beside(a, d, t).wait_send()
+                across(a, d, t).wait_send()
+                onward(a, d, t).wait_send()
+
+
+def feed(devices, hidden, chosen, chooser, down, up, frozen, self_rows):
+    rows, columns = chosen.shape
+    padded = chooser.shape[0]
+    vmem, anywhere = pl.BlockSpec(memory_space=pltpu.VMEM), pl.BlockSpec(memory_space=pl.ANY)
+    shape = lambda *dims: jax.ShapeDtypeStruct(dims, jnp.bfloat16)
+    return pl.pallas_call(
+        functools.partial(feed_kernel, devices),
+        in_specs=[vmem, vmem, vmem, anywhere, anywhere, anywhere, anywhere],
+        out_specs=[anywhere] * 4,
+        out_shape=[
+            shape(up.shape[0] * devices, columns),
+            shape(*frozen.shape),
+            shape(*self_rows.shape),
+            shape(padded, columns),
+        ],
+        scratch_shapes=[
+            pltpu.VMEM((down.shape[0] * devices, columns), jnp.bfloat16),
+            pltpu.VMEM((rows, columns), jnp.float32),
+            pltpu.VMEM((padded, columns), jnp.bfloat16),
+            pltpu.SemaphoreType.DMA((8, 2, 2, devices // 2)),
+            pltpu.SemaphoreType.DMA((2, 3, devices)),
+            pltpu.SemaphoreType.DMA((5,)),
+        ],
+        compiler_params=pltpu.CompilerParams(
+            collective_id=0, has_side_effects=True, vmem_limit_bytes=40 * 1024 * 1024
+        ),
+        name="feed",
+    )(hidden, chosen, chooser, down, up, frozen, self_rows)
+
+
 def on_device(
     hidden,
     frozen_query_rows,
@@ -146,15 +376,26 @@
         .transpose(0, 2, 1, 3)
         .reshape(slots * HEAD_GROUP, kv_width)
     )
-    frozen = exchange(frozen)
-    self_rows = exchange(place(jnp.concatenate([answer_row_key, answer_row_value], 1)))
-
-    down = lax.all_gather(adapter_down_weight, "score", axis=0, tiled=True)
-    up = lax.all_gather(adapter_up_weight, "score", axis=0, tiled=True)
+    pitch = -(-capacity // 16) * 16
+    wide_slot = slot // capacity * pitch + slot % capacity
+    wide_ids = jnp.arange(devices * pitch, dtype=jnp.int32)
+    wide = (wide_ids[:, None] == wide_slot[None, :]).astype(jnp.bfloat16)
+    self_rows = jnp.dot(
+        wide,
+        jnp.concatenate([answer_row_key, answer_row_value], 1),
+        preferred_element_type=jnp.float32,
+    ).astype(jnp.bfloat16)
     column_owner = jnp.arange(column_list, dtype=jnp.int32) // ADAPTER_RANK
-    chosen = row_checkpoint_index[:, None] == column_owner[None, :]
-    inner = jnp.dot(hidden, down, preferred_element_type=jnp.float32)
-    masked = exchange(place(jnp.where(chosen, inner, 0.0).astype(jnp.bfloat16)))
+    chosen = (row_checkpoint_index[:, None] == column_owner[None, :]).astype(jnp.float32)
+    up, frozen, self_rows, masked = feed(
+        devices, hidden, chosen, wide, adapter_down_weight, adapter_up_weight, frozen, self_rows
+    )
+
+    def tight(spaced):
+        parts = spaced.reshape(devices, pitch, spaced.shape[1])[:, :capacity]
+        return parts.reshape(slots, spaced.shape[1])
+
+    self_rows, masked = tight(self_rows), tight(masked)
 
     here = lax.axis_index("score")
     local_req = jnp.sum(jnp.where(request_device_owner == here, req_ids, 0))

time: 257 us -> 202 us (0.79)
  waiting for transfers between devices: 166 us -> 32 us
  Pallas kernels: 25.2 us -> 143 us
  starting transfers between devices: 24.4 us -> 4.54 us
  between operations: 15.5 us -> 2.16 us
  matrix products: 7.82 us -> 0.84 us
  local copies, waits for them, and re-layouts: 10.6 us -> 13.3 us
    pallas_call x0 -> x1, Pallas kernels: none -> 117 us  [feed(): pl.pallas_call(functools.partial(feed_kernel, devices), in_specs=[vmem, v...]
    all_gather x2 -> x0, waiting for transfers between devices: 77.8 us -> none  [the longest x1 77.8 us: on_device(): down = lax.all_gather(adapter_down_weight, 'score', axis=0, tiled=True)]
    all_to_all x4 -> x1, waiting for transfers between devices: 86.9 us -> 32 us  [exchange(): lax.all_to_all(parts, 'score', split_axis=0, concat_axis=0, tiled=True)]
    all_to_all x4 -> x1, starting transfers between devices: 24.3 us -> 4.54 us  [exchange(): lax.all_to_all(parts, 'score', split_axis=0, concat_axis=0, tiled=True)]
    dot_general x3 -> x1, matrix products: 7.82 us -> 0.56 us  [place(): jnp.dot(chooser, value_rows, preferred_element_type=jnp.float32)]
    unnamed x15 -> x31, local copies, waits for them, and re-layouts: 5.51 us -> 9.35 us
  transfers between devices with their start and end apart: 6 -> 1, of which waited for: 5 -> 1; matrix products, arithmetic and copies ran while one was open for 6% -> 0% of each run, Pallas kernels for 0% -> 0%
where the time goes in v2:
time: 202 us; the launch traced here: 199 us
  Pallas kernels  143 us (71%)
  waiting for transfers between devices  32 us (16%)
  local copies, waits for them, and re-layouts  13.3 us (7%)
  starting transfers between devices  4.54 us (2%)
  other arithmetic  2.97 us (1%)
  between operations  2.16 us (1%)
    pallas_call x1, Pallas kernels, feed(): pl.pallas_call(functools.partial(feed_kernel, devices), in_specs=[vmem, v...  117 us
    all_to_all x1, waiting for transfers between devices, exchange(): lax.all_to_all(parts, 'score', split_axis=0, concat_axis=0, tiled=True)  32 us
    pallas_call x1, Pallas kernels, attend(): pl.pallas_call(attend_kernel, grid=(KEY_VALUE_HEADS,), in_specs=[pl.Block...  25.8 us
    unnamed x31, local copies, waits for them, and re-layouts  9.35 us
    all_to_all x1, starting transfers between devices, exchange(): lax.all_to_all(parts, 'score', split_axis=0, concat_axis=0, tiled=True)  4.54 us
  transfers between devices with their start and end apart: 1, of which 1 were waited for; matrix products, arithmetic and copies ran while one was open for 0% of the time, Pallas kernels for 0%

profile of v2, /device:TPU:0, one launch (start us, length us, event | category | flops | bytes accessed | tf_op | source)
XLA Modules:
  0.0 198.6 jit_solution(15451256047385842494)
XLA Ops:
  0.0 0.9 select_reduce_fusion.1
  0.9 0.1 fusion.6
  1.0 0.2 reduce_window_sum.11
  1.2 0.2 select_reduce_fusion
  1.5 0.6 fusion
  2.1 0.0 copy-start.11
  2.1 0.0 copy-start.2
  2.1 0.3 copy.14
  2.4 0.5 copy-done.9
  2.9 0.1 copy-done.10
  3.0 0.3 convolution_convert_fusion.1.self_ref
  3.3 0.1 compare_convert_fusion.chosen_ref
  3.4 0.4 copy-done.2
  3.8 0.1 copy-done.6
  3.9 0.1 copy-done.8
  3.9 117.0 %feed.1 = (bf16[4096,512]{1,0:T(8,128)(2,1)S(1)}, bf16[1536,512]{1,0:T(8,128)(2,1)S(1)}, bf16[256,1024]{1,0:T(8,128)(2,1)S(1)}, bf16[256,512]{1,0:T(8,128)(2,1)S(1)}) custom-call(bf16[128,8192]{1,0:T(8,128)(2,1)S(1)} %copy-done.2, f32[128,512]{1,0:T(8,128)S(1)} %compare_convert_fusion.chosen_ref, bf16[256,128]{1,0:T(8,128)(2,1)S(1)} %fusion.4.chooser_ref, ...), custom_call_target="tpu_custom_call" | custom-call | tf_op jit(solution)/shard_map/feed/pallas_call | solution.py:306
  120.9 1.9 copy-done.1
  122.9 1.2 copy-done.4
  124.1 0.7 copy-done.7
  124.8 0.1 reshape.136.self_key_ref.self_value_ref
  124.9 1.0 reshape.134.masked_ref
  125.9 0.6 fusion.12
  128.4 0.7 dynamic-slice_bitcast_fusion
  129.1 0.1 select_reduce_fusion.2
  129.3 0.6 dynamic_slice.9
  129.9 0.7 select_bitcast_fusion
  130.6 1.4 copy-done.5
  132.0 25.8 %attend.1 = bf16[1536,512]{1,0:T(8,128)(2,1)} custom-call(bf16[1536,512]{1,0:T(8,128)(2,1)S(1)} %copy-done.5, bf16[192,512]{1,0:T(8,128)(2,1)S(1)} %reshape.134.masked_ref, bf16[4096,512]{1,0:T(8,128)(2,1)} %copy-done.1, bf16[12,128,512]{2,1,0:T(8,128)(2,1)S(1)} %copy-done.3, bf16[12,128,512]{2,1,0:T(8,128)(2,1)} %value_ref.1, ...), custom_call_target="tpu_custom_call" | custom-call | tf_op jit(solution)/shard_map/attend/pallas_call | solution.py:80
  157.8 4.5 %all-to-all-start = ((bf16[16,96,512]{2,1,0:T(8,128)(2,1)}), bf16[16,96,512]{2,1,0:T(8,128)(2,1)S(1)}, u32[]{:S(2)}, u32[]{:S(2)}) async-start(bf16[16,96,512]{2,1,0:T(8,128)(2,1)} %bitcast.7), calls=%async_computation | async-start | bytes 3145728 | tf_op jit(solution)/shard_map/all_to_all | solution.py:370
  162.3 32.0 %all-to-all-done = bf16[16,96,512]{2,1,0:T(8,128)(2,1)S(1)} async-done(((bf16[16,96,512]{2,1,0:T(8,128)(2,1)}), bf16[16,96,512]{2,1,0:T(8,128)(2,1)S(1)}, u32[]{:S(2)}, u32[]{:S(2)}) %all-to-all-start) | async-done | bytes 1572896 | tf_op jit(solution)/shard_map/all_to_all | solution.py:370
  194.3 1.6 gather_fusion
  195.9 2.6 %copy.19 = bf16[16,8,32,128]{3,1,2,0:T(8,128)(2,1)} copy(bf16[16,8,32,128]{3,2,1,0:T(8,128)(2,1)} %bitcast.42) | data formatting | bytes 2097152
  (24 shorter events, 0.1 us)
Async XLA Ops:
  0.0 1.5 copy-start
  2.0 0.9 copy-start.9
  2.0 1.0 copy-start.10
  2.1 1.2 copy-start.11
  2.1 1.7 copy-start.2
  2.1 1.8 copy-start.6
  2.1 1.8 copy-start.8
  3.9 121.9 %copy-start.12 = (s32[16]{0:T(128)S(1)}, s32[16]{0:T(128)}, u32[]{:S(2)}) copy-start(s32[16]{0:T(128)} %param.19) | copy-start | bytes 196
  3.9 125.3 %copy-start.13 = (s32[16]{0:T(128)S(1)}, s32[16]{0:T(128)}, u32[]{:S(2)}) copy-start(s32[16]{0:T(128)} %param.21) | copy-start | bytes 196
  3.9 126.6 %copy-start.3 = (bf16[12,128,512]{2,1,0:T(8,128)(2,1)S(1)}, bf16[12,128,512]{2,1,0:T(8,128)(2,1)}, u32[]{:S(2)}) copy-start(bf16[12,128,512]{2,1,0:T(8,128)(2,1)} %key_ref.1) | copy-start | bytes 4718596
  120.9 1.9 copy-start.1
  122.9 1.2 copy-start.4
  124.1 0.7 copy-start.7
  130.6 1.4 copy-start.5
  157.8 36.5 %all-to-all-start = ((bf16[16,96,512]{2,1,0:T(8,128)(2,1)}), bf16[16,96,512]{2,1,0:T(8,128)(2,1)S(1)}, u32[]{:S(2)}, u32[]{:S(2)}) async-start(bf16[16,96,512]{2,1,0:T(8,128)(2,1)} %bitcast.7), calls=%async_computation | async-start | bytes 3145728 | tf_op jit(solution)/shard_map/all_to_all | solution.py:370

commit v3 on v2

--- a/solution.py
+++ b/solution.py
@@ -17,6 +17,8 @@
 TOKEN_SPAN = MAXB * BLOCK_TOKENS
 SCORE_SCALE = 1.4426950408889634 / HEAD_SIZE**0.5
 CHUNK = 256
+LAG = 2
+PEERS = 1
 
 
 def attend_kernel(
@@ -149,6 +151,10 @@
         span = pl.ds(pl.multiple_of(owner * rows, rows), rows)
         if quarter is None:
             return fulls[a].at[span, :]
+        if rows % 64 == 0:
+            size = rows // 4
+            first = pl.multiple_of(owner * rows + quarter * size, size)
+            return fulls[a].at[pl.ds(first, size), :]
         return fulls[a].at[span, pl.ds(pl.multiple_of(quarter * parts, parts), parts)]
 
     def origin(d, t):
@@ -208,28 +214,27 @@
             ring(a, d, 0).start()
         whole(a).start()
 
-    def circle(a):
-        @pl.loop(0, chips - 1)
-        def _(t):
+    def step(a, t):
+        for d in range(2):
+            ring(a, d, t).wait_recv()
+
+            @pl.when(t < chips - 2)
+            def _():
+                ring(a, d, t + 1).start()
+
+            across(a, d, t + 1).start()
+            beside(a, d, t + 1).start()
+
+        @pl.when(t > 0)
+        def _():
             for d in range(2):
-                ring(a, d, t).wait_recv()
-
-                @pl.when(t < chips - 2)
-                def _():
-                    ring(a, d, t + 1).start()
-
-                across(a, d, t + 1).start()
-                beside(a, d, t + 1).start()
-            if a == 0:
-                for extra in range(2):
-                    rows_to(0, 2 * t + 1 + extra).start()
-                    rows_to(1, 2 * t + 1 + extra).start()
-
-            @pl.when(t > 0)
-            def _():
-                for d in range(2):
-                    across(a, d, t).wait_recv()
-                    onward(a, d, t).start()
+                across(a, d, t).wait_recv()
+                onward(a, d, t).start()
+
+    def send_rows(turn):
+        offset = lax.rem(turn + devices // 2 - 1, devices - 1) + 1
+        rows_to(0, offset).start()
+        rows_to(1, offset).start()
 
     def finish(a):
         for d in range(2):
@@ -244,10 +249,24 @@
                 onward(a, d, t).wait_recv()
 
     begin(0)
-    rows_to(0, devices - 1).start()
-    rows_to(1, devices - 1).start()
-    circle(0)
     begin(1)
+    lag = min(LAG, chips - 1)
+
+    @pl.loop(0, chips - 1)
+    def _(t):
+        step(0, t)
+
+        @pl.when(t >= lag)
+        def _():
+            step(1, t - lag)
+
+        for extra in range(PEERS):
+            send_rows(PEERS * t + extra)
+
+    @pl.loop(PEERS * (chips - 1), devices - 1)
+    def _(turn):
+        send_rows(turn)
+
     finish(0)
 
     total[...] = jnp.zeros_like(total)
@@ -270,7 +289,10 @@
     def _(offset):
         rows_to(2, offset).start()
 
-    circle(1)
+    @pl.loop(chips - 1 - lag, chips - 1)
+    def _(t):
+        step(1, t)
+
     finish(1)
 
     for kind in range(3):
@@ -380,23 +402,11 @@
     wide_slot = slot // capacity * pitch + slot % capacity
     wide_ids = jnp.arange(devices * pitch, dtype=jnp.int32)
     wide = (wide_ids[:, None] == wide_slot[None, :]).astype(jnp.bfloat16)
-    self_rows = jnp.dot(
-        wide,
-        jnp.concatenate([answer_row_key, answer_row_value], 1),
-        preferred_element_type=jnp.float32,
-    ).astype(jnp.bfloat16)
+    self_rows = place(jnp.concatenate([answer_row_key, answer_row_value], 1)).reshape(
+        slots * 2 * KEY_VALUE_HEADS, HEAD_SIZE
+    )
     column_owner = jnp.arange(column_list, dtype=jnp.int32) // ADAPTER_RANK
     chosen = (row_checkpoint_index[:, None] == column_owner[None, :]).astype(jnp.float32)
-    up, frozen, self_rows, masked = feed(
-        devices, hidden, chosen, wide, adapter_down_weight, adapter_up_weight, frozen, self_rows
-    )
-
-    def tight(spaced):
-        parts = spaced.reshape(devices, pitch, spaced.shape[1])[:, :capacity]
-        return parts.reshape(slots, spaced.shape[1])
-
-    self_rows, masked = tight(self_rows), tight(masked)
-
     here = lax.axis_index("score")
     local_req = jnp.sum(jnp.where(request_device_owner == here, req_ids, 0))
     order = lax.dynamic_index_in_dim(request_block_table, local_req, 0, keepdims=False)
@@ -405,6 +415,14 @@
     place_of = jnp.sum(jnp.where(order[None, :] == blocks[:, None], blocks[None, :], 0), 1)
     position = place_of[:, None] * BLOCK_TOKENS + jnp.arange(BLOCK_TOKENS, dtype=jnp.int32)[None, :]
     bias = jnp.where(position < length, 0.0, -jnp.inf).astype(jnp.float32).reshape(1, TOKEN_SPAN)
+
+    frozen, bias = lax.optimization_barrier((frozen, bias))
+    up, frozen, self_rows, masked = feed(
+        devices, hidden, chosen, wide, adapter_down_weight, adapter_up_weight, frozen, self_rows
+    )
+
+    self_rows = self_rows.reshape(slots, 2 * kv_width)
+    masked = masked.reshape(devices, pitch, column_list)[:, :capacity].reshape(slots, column_list)
 
     answer = attend(frozen, masked, up, paged_key_blocks, paged_value_blocks, self_rows, bias)
     returned = exchange(answer).reshape(slots, HEAD_GROUP, kv_width)[slot]

time: 202 us -> 191 us (0.946)
  the two profiles are of different devices: /device:TPU:0 before, /device:TPU:15 now
where the time goes in v3:
time: 191 us; the launch traced here: 190 us
  Pallas kernels  118 us (62%)
  waiting for transfers between devices  36.2 us (19%)
  local copies, waits for them, and re-layouts  20.4 us (11%)
  starting transfers between devices  6 us (3%)
  other arithmetic  5.46 us (3%)
  between operations  2.09 us (1%)
    pallas_call x1, Pallas kernels, feed(): pl.pallas_call(functools.partial(feed_kernel, devices), in_specs=[vmem, v...  92.4 us
    all_to_all x1, waiting for transfers between devices, exchange(): lax.all_to_all(parts, 'score', split_axis=0, concat_axis=0, tiled=True)  36.2 us
    pallas_call x1, Pallas kernels, attend(): pl.pallas_call(attend_kernel, grid=(KEY_VALUE_HEADS,), in_specs=[pl.Block...  25.9 us
    unnamed x27, local copies, waits for them, and re-layouts  13.5 us
    all_to_all x1, starting transfers between devices, exchange(): lax.all_to_all(parts, 'score', split_axis=0, concat_axis=0, tiled=True)  6 us
  transfers between devices with their start and end apart: 1, of which 1 were waited for; matrix products, arithmetic and copies ran while one was open for 0% of the time, Pallas kernels for 0%

profile of v3, /device:TPU:15, one launch (start us, length us, event | category | flops | bytes accessed | tf_op | source)
XLA Modules:
  0.0 189.9 jit_solution(13578389858269512589)
XLA Ops:
  0.0 1.4 fusion.12
  3.3 0.7 dynamic-slice_bitcast_fusion
  4.0 0.1 select_reduce_fusion.2
  4.2 1.2 dynamic_slice.9
  5.4 0.7 select_bitcast_fusion
  6.1 0.8 select_reduce_fusion.1
  7.1 0.2 reduce_window_sum.11
  7.2 0.2 select_reduce_fusion
  7.4 0.6 fusion.11
  8.0 0.6 fusion
  8.6 0.3 copy.14
  8.9 0.5 copy-done.10
  9.5 1.0 convolution_convert_fusion.1
  10.5 1.2 reshape.133.self_ref
  11.7 0.6 fusion.4.chooser_ref
  12.3 0.7 compare_convert_fusion.chosen_ref
  13.1 1.6 copy-done.2
  14.7 0.9 copy-done.8
  15.6 92.4 %feed.1 = (bf16[4096,512]{1,0:T(8,128)(2,1)S(1)}, bf16[1536,512]{1,0:T(8,128)(2,1)S(1)}, bf16[1536,128]{1,0:T(8,128)(2,1)S(1)}, bf16[256,512]{1,0:T(8,128)(2,1)S(1)}) custom-call(bf16[128,8192]{1,0:T(8,128)(2,1)S(1)} %copy-done.2, f32[128,512]{1,0:T(8,128)S(1)} %compare_convert_fusion.chosen_ref, bf16[256,128]{1,0:T(8,128)(2,1)S(1)} %fusion.4.chooser_ref, ...), custom_call_target="tpu_custom_call" | custom-call | tf_op jit(solution)/shard_map/feed/pallas_call | solution.py:328
  108.1 1.9 %copy-done.1 = bf16[4096,512]{1,0:T(8,128)(2,1)} copy-done((bf16[4096,512]{1,0:T(8,128)(2,1)}, bf16[4096,512]{1,0:T(8,128)(2,1)S(1)}, u32[]{:S(2)}) %copy-start.1) | copy-done | bytes 4194328
  110.0 1.2 copy-done.4
  111.2 0.7 copy-done.7
  111.9 0.7 copy-done.9
  112.6 1.2 reshape.136.self_key_ref.self_value_ref
  113.8 1.0 reshape.135.masked_ref
  114.8 1.4 copy-done.3
  116.2 1.4 copy-done.5
  117.6 25.9 %attend.1 = bf16[1536,512]{1,0:T(8,128)(2,1)} custom-call(bf16[1536,512]{1,0:T(8,128)(2,1)S(1)} %copy-done.5, bf16[192,512]{1,0:T(8,128)(2,1)S(1)} %reshape.135.masked_ref, bf16[4096,512]{1,0:T(8,128)(2,1)} %copy-done.1, bf16[12,128,512]{2,1,0:T(8,128)(2,1)S(1)} %copy-done.3, bf16[12,128,512]{2,1,0:T(8,128)(2,1)} %value_ref.1, ...), custom_call_target="tpu_custom_call" | custom-call | tf_op jit(solution)/shard_map/attend/pallas_call | solution.py:82
  143.5 6.0 %all-to-all-start = ((bf16[16,96,512]{2,1,0:T(8,128)(2,1)}), bf16[16,96,512]{2,1,0:T(8,128)(2,1)S(1)}, u32[]{:S(2)}, u32[]{:S(2)}) async-start(bf16[16,96,512]{2,1,0:T(8,128)(2,1)} %bitcast.6), calls=%async_computation | async-start | bytes 3145728 | tf_op jit(solution)/shard_map/all_to_all | solution.py:392
  149.5 36.2 %all-to-all-done = bf16[16,96,512]{2,1,0:T(8,128)(2,1)S(1)} async-done(((bf16[16,96,512]{2,1,0:T(8,128)(2,1)}), bf16[16,96,512]{2,1,0:T(8,128)(2,1)S(1)}, u32[]{:S(2)}, u32[]{:S(2)}) %all-to-all-start) | async-done | bytes 1572896 | tf_op jit(solution)/shard_map/all_to_all | solution.py:392
  185.7 1.6 gather_fusion
  187.3 2.6 %copy.19 = bf16[16,8,32,128]{3,1,2,0:T(8,128)(2,1)} copy(bf16[16,8,32,128]{3,2,1,0:T(8,128)(2,1)} %bitcast.39) | data formatting | bytes 2097152
  (21 shorter events, 0.2 us)
Async XLA Ops:
  0.0 8.0 %copy-start = (bf16[128,4096]{1,0:T(8,128)(2,1)S(1)}, bf16[128,4096]{1,0:T(8,128)(2,1)}, u32[]{:S(2)}) copy-start(bf16[128,4096]{1,0:T(8,128)(2,1)} %param.14) | copy-start | bytes 3145732
  8.6 0.9 copy-start.10
  8.6 1.0 copy-start.11
  8.9 4.2 %copy-start.6 = (bf16[512,512]{1,0:T(8,128)(2,1)S(1)}, bf16[512,512]{1,0:T(8,128)(2,1)}, u32[]{:S(2)}) copy-start(bf16[512,512]{1,0:T(8,128)(2,1)} %down_ref.1) | copy-start | bytes 1572868
  13.1 1.6 copy-start.2
  14.7 0.9 copy-start.8
  108.0 1.9 %copy-start.1 = (bf16[4096,512]{1,0:T(8,128)(2,1)}, bf16[4096,512]{1,0:T(8,128)(2,1)S(1)}, u32[]{:S(2)}) copy-start(bf16[4096,512]{1,0:T(8,128)(2,1)S(1)} %get-tuple-element.14.up_ref) | copy-start | bytes 12582916
  110.0 1.2 copy-start.4
  111.2 0.7 copy-start.7
  111.9 0.7 copy-start.9
  114.8 1.4 copy-start.3
  116.2 1.4 copy-start.5
  143.5 42.2 %all-to-all-start = ((bf16[16,96,512]{2,1,0:T(8,128)(2,1)}), bf16[16,96,512]{2,1,0:T(8,128)(2,1)S(1)}, u32[]{:S(2)}, u32[]{:S(2)}) async-start(bf16[16,96,512]{2,1,0:T(8,128)(2,1)} %bitcast.6), calls=%async_computation | async-start | bytes 3145728 | tf_op jit(solution)/shard_map/all_to_all | solution.py:392

commit v4 on v3

--- a/solution.py
+++ b/solution.py
@@ -22,10 +22,41 @@
 
 
 def attend_kernel(
-    frozen_ref, masked_ref, up_ref, key_ref, value_ref, self_key_ref, self_value_ref, bias_ref,
-    out_ref, change_ref,
+    devices, frozen_ref, masked_ref, up_ref, key_ref, value_ref, self_key_ref, self_value_ref, bias_ref,
+    out_ref, change_ref, answer_ref, sems, local_sems,
 ):
     slots = masked_ref.shape[0]
+    share = slots * HEAD_GROUP // devices
+    here = lax.axis_index("score")
+    turn = pl.program_id(0)
+    barrier = pltpu.get_barrier_semaphore()
+
+    @pl.when(turn == 0)
+    def _():
+        @pl.loop(1, devices)
+        def _(offset):
+            pl.semaphore_signal(
+                barrier, inc=1, device_id={"score": lax.rem(here + offset, devices)},
+                device_id_type=pl.DeviceIdType.MESH,
+            )
+
+    def back(g, offset):
+        peer = lax.rem(here + offset, devices)
+        return pltpu.make_async_remote_copy(
+            src_ref=answer_ref.at[g, pl.ds(pl.multiple_of(peer * share, share), share), :],
+            dst_ref=out_ref.at[g, pl.ds(pl.multiple_of(here * share, share), share), :],
+            send_sem=sems.at[0, g, offset],
+            recv_sem=sems.at[1, g, offset],
+            device_id={"score": peer},
+            device_id_type=pl.DeviceIdType.MESH,
+        )
+
+    def stay(g):
+        span = pl.ds(pl.multiple_of(here * share, share), share)
+        return pltpu.make_async_copy(
+            answer_ref.at[g, span, :], out_ref.at[g, span, :], local_sems.at[g]
+        )
+
     for head in range(HEAD_GROUP):
         change_ref[pl.ds(head, slots, stride=HEAD_GROUP), :] = lax.dot_general(
             masked_ref[...],
@@ -70,17 +101,36 @@
             (weights * inverse).astype(jnp.bfloat16), values, preferred_element_type=jnp.float32
         )
         self_weight = (self_weight * inverse).astype(jnp.bfloat16).astype(jnp.float32)
-        out_ref[part, :] = (mixed + self_weight * spread(self_value_ref[part_slots, :])).astype(
+        answer_ref[turn, part, :] = (mixed + self_weight * spread(self_value_ref[part_slots, :])).astype(
             jnp.bfloat16
         )
 
-
-def attend(frozen, masked, up, keys, values, self_rows, bias):
+    @pl.when(turn == 0)
+    def _():
+        pl.semaphore_wait(barrier, devices - 1)
+
+    stay(turn).start()
+
+    @pl.loop(0, devices - 1)
+    def _(peer):
+        back(turn, lax.rem(peer + devices // 2 - 1, devices - 1) + 1).start()
+
+    @pl.when(turn == KEY_VALUE_HEADS - 1)
+    def _():
+        for g in range(KEY_VALUE_HEADS):
+            stay(g).wait()
+
+            @pl.loop(1, devices)
+            def _(offset):
+                back(g, offset).wait()
+
+
+def attend(devices, frozen, masked, up, keys, values, self_rows, bias):
     slots, columns = masked.shape
     items = slots * HEAD_GROUP
     head_blocks = (MAXB, BLOCK_TOKENS, HEAD_SIZE)
     return pl.pallas_call(
-        attend_kernel,
+        functools.partial(attend_kernel, devices),
         grid=(KEY_VALUE_HEADS,),
         in_specs=[
             pl.BlockSpec((items, HEAD_SIZE), lambda g: (0, g)),
@@ -92,10 +142,17 @@
             pl.BlockSpec((slots, HEAD_SIZE), lambda g: (0, KEY_VALUE_HEADS + g)),
             pl.BlockSpec((1, TOKEN_SPAN), lambda g: (0, 0)),
         ],
-        out_specs=pl.BlockSpec((items, HEAD_SIZE), lambda g: (0, g)),
-        out_shape=jax.ShapeDtypeStruct((items, KEY_VALUE_HEADS * HEAD_SIZE), jnp.bfloat16),
-        scratch_shapes=[pltpu.VMEM((items, HEAD_SIZE), jnp.float32)],
-        compiler_params=pltpu.CompilerParams(vmem_limit_bytes=48 * 1024 * 1024),
+        out_specs=pl.BlockSpec(memory_space=pl.ANY),
+        out_shape=jax.ShapeDtypeStruct((KEY_VALUE_HEADS, items, HEAD_SIZE), jnp.bfloat16),
+        scratch_shapes=[
+            pltpu.VMEM((items, HEAD_SIZE), jnp.float32),
+            pltpu.VMEM((KEY_VALUE_HEADS, items, HEAD_SIZE), jnp.bfloat16),
+            pltpu.SemaphoreType.DMA((2, KEY_VALUE_HEADS, devices)),
+            pltpu.SemaphoreType.DMA((KEY_VALUE_HEADS,)),
+        ],
+        compiler_params=pltpu.CompilerParams(
+            collective_id=1, has_side_effects=True, vmem_limit_bytes=48 * 1024 * 1024
+        ),
         name="attend",
     )(frozen, masked, up, keys, values, self_rows, self_rows, bias)
 
@@ -387,11 +444,6 @@
             jnp.bfloat16
         )
 
-    def exchange(filled):
-        parts = filled.reshape(devices, filled.shape[0] // devices, filled.shape[1])
-        moved = lax.all_to_all(parts, "score", split_axis=0, concat_axis=0, tiled=True)
-        return moved.reshape(filled.shape)
-
     frozen = (
         place(frozen_query_rows)
         .reshape(slots, KEY_VALUE_HEADS, HEAD_GROUP, HEAD_SIZE)
@@ -424,13 +476,11 @@
     self_rows = self_rows.reshape(slots, 2 * kv_width)
     masked = masked.reshape(devices, pitch, column_list)[:, :capacity].reshape(slots, column_list)
 
-    answer = attend(frozen, masked, up, paged_key_blocks, paged_value_blocks, self_rows, bias)
-    returned = exchange(answer).reshape(slots, HEAD_GROUP, kv_width)[slot]
-    return (
-        returned.reshape(rows, HEAD_GROUP, KEY_VALUE_HEADS, HEAD_SIZE)
-        .transpose(0, 2, 1, 3)
-        .reshape(rows, width)
-    )
+    returned = attend(
+        devices, frozen, masked, up, paged_key_blocks, paged_value_blocks, self_rows, bias
+    )
+    returned = returned.reshape(KEY_VALUE_HEADS, slots, HEAD_GROUP, HEAD_SIZE)[:, slot]
+    return returned.transpose(1, 0, 2, 3).reshape(rows, width)
 
 
 def solution(mesh):

time: 191 us -> 168 us (0.88)
  the two profiles are of different devices: /device:TPU:15 before, /device:TPU:0 now
where the time goes in v4:
time: 168 us
  Pallas kernels  139 us (83%)
  local copies, waits for them, and re-layouts  20.6 us (12%)
  other arithmetic  4.29 us (3%)
  between operations  2.12 us (1%)
    pallas_call x1, Pallas kernels, feed(): pl.pallas_call(functools.partial(feed_kernel, devices), in_specs=[vmem, v...  90.4 us
    pallas_call x1, Pallas kernels, attend(): pl.pallas_call(functools.partial(attend_kernel, devices), grid=(KEY_VALUE...  48.7 us
    unnamed x27, local copies, waits for them, and re-layouts  13.5 us

profile of v4, /device:TPU:0, one launch (start us, length us, event | category | flops | bytes accessed | tf_op | source)
XLA Modules:
  0.0 167.7 jit_solution(12870313547656850084)
XLA Ops:
  0.0 1.4 fusion.12
  3.3 0.7 dynamic-slice_bitcast_fusion
  4.0 0.1 select_reduce_fusion.2
  4.1 1.2 dynamic_slice.9
  5.4 0.7 select_bitcast_fusion
  6.1 0.8 select_reduce_fusion.1
  7.0 0.1 fusion.5
  7.1 0.2 reduce_window_sum.11
  7.2 0.2 select_reduce_fusion
  7.4 0.6 fusion
  8.0 0.0 copy-start.10
  8.0 0.3 copy.14
  8.4 0.0 copy-start.6
  8.4 0.5 copy-done.10
  8.9 0.1 copy-done.11
  9.0 1.0 convolution_convert_fusion.1
  10.0 1.2 reshape.130.self_ref
  11.2 0.7 compare_convert_fusion.chosen_ref
  12.0 1.6 copy-done.2
  13.6 0.9 copy-done.8
  14.5 90.4 %feed.1 = (bf16[4096,512]{1,0:T(8,128)(2,1)S(1)}, bf16[1536,512]{1,0:T(8,128)(2,1)S(1)}, bf16[1536,128]{1,0:T(8,128)(2,1)S(1)}, bf16[256,512]{1,0:T(8,128)(2,1)S(1)}) custom-call(bf16[128,8192]{1,0:T(8,128)(2,1)S(1)} %copy-done.2, f32[128,512]{1,0:T(8,128)S(1)} %compare_convert_fusion.chosen_ref, bf16[256,128]{1,0:T(8,128)(2,1)S(1)} %fusion.4.chooser_ref, ...), custom_call_target="tpu_custom_call" | custom-call | tf_op jit(solution)/shard_map/feed/pallas_call | solution.py:385
  105.0 1.9 %copy-done.1 = bf16[4096,512]{1,0:T(8,128)(2,1)} copy-done((bf16[4096,512]{1,0:T(8,128)(2,1)}, bf16[4096,512]{1,0:T(8,128)(2,1)S(1)}, u32[]{:S(2)}) %copy-start.1) | copy-done | bytes 4194328
  106.9 1.2 copy-done.4
  108.1 0.7 copy-done.7
  108.8 0.7 copy-done.9
  109.5 1.2 reshape.133.self_key_ref.self_value_ref
  110.7 1.0 reshape.132.masked_ref
  111.7 1.4 copy-done.3
  113.1 1.4 copy-done.5
  114.5 48.7 %attend.1 = bf16[4,1536,128]{2,1,0:T(8,128)(2,1)S(1)} custom-call(bf16[1536,512]{1,0:T(8,128)(2,1)S(1)} %copy-done.5, bf16[192,512]{1,0:T(8,128)(2,1)S(1)} %reshape.132.masked_ref, bf16[4096,512]{1,0:T(8,128)(2,1)} %copy-done.1, bf16[12,128,512]{2,1,0:T(8,128)(2,1)S(1)} %copy-done.3, bf16[12,128,512]{2,1,0:T(8,128)(2,1)} %value_ref.1, ...), custom_call_target="tpu_custom_call" | custom-call | tf_op jit(solution)/shard_map/attend/pallas_call | solution.py:132
  163.2 1.9 %gather_fusion = bf16[128,4,8,128]{3,2,1,0:T(8,128)(2,1)} fusion(bf16[4,192,8,128]{3,2,1,0:T(8,128)(2,1)S(1)} %bitcast.32, s32[1024]{0:T(1024)S(1)} %pad_clamp_fusion), kind=kCustom, calls=%fused_computation | custom fusion | bytes 2097664 | tf_op jit(solution)/shard_map/gather | solution.py:482
  165.1 2.6 %copy.19 = bf16[16,8,32,128]{3,1,2,0:T(8,128)(2,1)} copy(bf16[16,8,32,128]{3,2,1,0:T(8,128)(2,1)} %bitcast.35) | data formatting | bytes 2097152
  (19 shorter events, 0.1 us)
Async XLA Ops:
  0.0 7.4 %copy-start = (bf16[128,4096]{1,0:T(8,128)(2,1)S(1)}, bf16[128,4096]{1,0:T(8,128)(2,1)}, u32[]{:S(2)}) copy-start(bf16[128,4096]{1,0:T(8,128)(2,1)} %param.14) | copy-start | bytes 3145732
  8.0 0.9 copy-start.10
  8.0 1.0 copy-start.11
  8.4 3.6 %copy-start.6 = (bf16[512,512]{1,0:T(8,128)(2,1)S(1)}, bf16[512,512]{1,0:T(8,128)(2,1)}, u32[]{:S(2)}) copy-start(bf16[512,512]{1,0:T(8,128)(2,1)} %down_ref.1) | copy-start | bytes 1572868
  12.0 1.6 copy-start.2
  13.6 0.9 copy-start.8
  104.9 1.9 %copy-start.1 = (bf16[4096,512]{1,0:T(8,128)(2,1)}, bf16[4096,512]{1,0:T(8,128)(2,1)S(1)}, u32[]{:S(2)}) copy-start(bf16[4096,512]{1,0:T(8,128)(2,1)S(1)} %get-tuple-element.14.up_ref) | copy-start | bytes 12582916
  106.9 1.2 copy-start.4
  108.0 0.7 copy-start.7
  108.8 0.7 copy-start.9
  111.7 1.4 copy-start.3
  113.1 1.4 copy-start.5

commit v5 on v4

--- a/solution.py
+++ b/solution.py
@@ -22,7 +22,8 @@
 
 
 def attend_kernel(
-    devices, frozen_ref, masked_ref, up_ref, key_ref, value_ref, self_key_ref, self_value_ref, bias_ref,
+    devices, frozen_ref, masked_ref, up_ref, key_ref, value_ref, self_key_ref, self_value_ref,
+    owner_ref, table_ref, length_ref,
     out_ref, change_ref, answer_ref, sems, local_sems,
 ):
     slots = masked_ref.shape[0]
@@ -66,7 +67,15 @@
         )
     keys = key_ref[...].reshape(TOKEN_SPAN, HEAD_SIZE)
     values = value_ref[...].reshape(TOKEN_SPAN, HEAD_SIZE)
-    bias = bias_ref[...]
+    mine = owner_ref[...] == here
+    token = lax.broadcasted_iota(jnp.int32, (1, TOKEN_SPAN), 1)
+    block = lax.div(token, BLOCK_TOKENS)
+    position = lax.rem(token, BLOCK_TOKENS)
+    for j in range(MAXB):
+        stored = jnp.sum(jnp.where(mine, table_ref[:, j : j + 1], 0), 0, keepdims=True)
+        position += jnp.where(block == stored, j * BLOCK_TOKENS, 0)
+    length = jnp.sum(jnp.where(mine, length_ref[...], 0), 0, keepdims=True)
+    bias = jnp.where(position < length, 0.0, -jnp.inf)
 
     def spread(rows):
         wide = rows.astype(jnp.float32)[:, None, :]
@@ -125,7 +134,7 @@
                 back(g, offset).wait()
 
 
-def attend(devices, frozen, masked, up, keys, values, self_rows, bias):
+def attend(devices, frozen, masked, up, keys, values, self_rows, owner, table, length):
     slots, columns = masked.shape
     items = slots * HEAD_GROUP
     head_blocks = (MAXB, BLOCK_TOKENS, HEAD_SIZE)
@@ -140,7 +149,9 @@
             pl.BlockSpec(head_blocks, lambda g: (0, 0, g)),
             pl.BlockSpec((slots, HEAD_SIZE), lambda g: (0, g)),
             pl.BlockSpec((slots, HEAD_SIZE), lambda g: (0, KEY_VALUE_HEADS + g)),
-            pl.BlockSpec((1, TOKEN_SPAN), lambda g: (0, 0)),
+            pl.BlockSpec(owner.shape, lambda g: (0, 0)),
+            pl.BlockSpec(table.shape, lambda g: (0, 0)),
+            pl.BlockSpec(length.shape, lambda g: (0, 0)),
         ],
         out_specs=pl.BlockSpec(memory_space=pl.ANY),
         out_shape=jax.ShapeDtypeStruct((KEY_VALUE_HEADS, items, HEAD_SIZE), jnp.bfloat16),
@@ -154,7 +165,7 @@
             collective_id=1, has_side_effects=True, vmem_limit_bytes=48 * 1024 * 1024
         ),
         name="attend",
-    )(frozen, masked, up, keys, values, self_rows, self_rows, bias)
+    )(frozen, masked, up, keys, values, self_rows, self_rows, owner, table, length)
 
 
 def ring_chip(place, chips):
@@ -459,16 +470,6 @@
     )
     column_owner = jnp.arange(column_list, dtype=jnp.int32) // ADAPTER_RANK
     chosen = (row_checkpoint_index[:, None] == column_owner[None, :]).astype(jnp.float32)
-    here = lax.axis_index("score")
-    local_req = jnp.sum(jnp.where(request_device_owner == here, req_ids, 0))
-    order = lax.dynamic_index_in_dim(request_block_table, local_req, 0, keepdims=False)
-    length = lax.dynamic_index_in_dim(request_prefix_length, local_req, 0, keepdims=False)
-    blocks = jnp.arange(MAXB, dtype=jnp.int32)
-    place_of = jnp.sum(jnp.where(order[None, :] == blocks[:, None], blocks[None, :], 0), 1)
-    position = place_of[:, None] * BLOCK_TOKENS + jnp.arange(BLOCK_TOKENS, dtype=jnp.int32)[None, :]
-    bias = jnp.where(position < length, 0.0, -jnp.inf).astype(jnp.float32).reshape(1, TOKEN_SPAN)
-
-    frozen, bias = lax.optimization_barrier((frozen, bias))
     up, frozen, self_rows, masked = feed(
         devices, hidden, chosen, wide, adapter_down_weight, adapter_up_weight, frozen, self_rows
     )
@@ -477,7 +478,16 @@
     masked = masked.reshape(devices, pitch, column_list)[:, :capacity].reshape(slots, column_list)
 
     returned = attend(
-        devices, frozen, masked, up, paged_key_blocks, paged_value_blocks, self_rows, bias
+        devices,
+        frozen,
+        masked,
+        up,
+        paged_key_blocks,
+        paged_value_blocks,
+        self_rows,
+        request_device_owner[:, None],
+        request_block_table,
+        request_prefix_length[:, None],
     )
     returned = returned.reshape(KEY_VALUE_HEADS, slots, HEAD_GROUP, HEAD_SIZE)[:, slot]
     return returned.transpose(1, 0, 2, 3).reshape(rows, width)

time: 168 us -> 162 us (0.964)
  other arithmetic: 4.29 us -> 1.5 us
  between operations: 2.12 us -> 0.19 us
    unnamed x27 -> x32, local copies, waits for them, and re-layouts: 13.5 us -> 13.5 us
where the time goes in v5:
time: 162 us
  Pallas kernels  139 us (86%)
  local copies, waits for them, and re-layouts  19.4 us (12%)
    pallas_call x1, Pallas kernels, feed(): pl.pallas_call(functools.partial(feed_kernel, devices), in_specs=[vmem, v...  90.5 us
    pallas_call x1, Pallas kernels, attend(): pl.pallas_call(functools.partial(attend_kernel, devices), grid=(KEY_VALUE...  48.7 us
    unnamed x32, local copies, waits for them, and re-layouts  13.5 us

profile of v5, /device:TPU:0, one launch (start us, length us, event | category | flops | bytes accessed | tf_op | source)
XLA Modules:
  0.0 161.8 jit_solution(11618893446562745382)
XLA Ops:
  0.0 0.9 select_reduce_fusion.1
  0.9 0.1 fusion.5
  1.0 0.2 reduce_window_sum.11
  1.2 0.2 select_reduce_fusion
  1.4 0.6 fusion
  2.0 0.0 copy-start.11
  2.0 0.0 copy-start.12
  2.0 0.0 copy-start.13
  2.0 0.3 copy.18
  2.4 0.0 copy-start.6
  2.4 0.5 copy-done.11
  2.9 0.1 copy-done.12
  3.0 1.0 convolution_convert_fusion.1
  3.9 1.2 reshape.92.self_ref
  5.2 0.1 compare_convert_fusion.chosen_ref
  5.3 0.0 copy-start.2
  5.3 1.6 copy-done.2
  6.9 0.9 copy-done.8
  7.8 90.5 %feed.1 = (bf16[4096,512]{1,0:T(8,128)(2,1)S(1)}, bf16[1536,512]{1,0:T(8,128)(2,1)S(1)}, bf16[1536,128]{1,0:T(8,128)(2,1)S(1)}, bf16[256,512]{1,0:T(8,128)(2,1)S(1)}) custom-call(bf16[128,8192]{1,0:T(8,128)(2,1)S(1)} %copy-done.2, f32[128,512]{1,0:T(8,128)S(1)} %compare_convert_fusion.chosen_ref, bf16[256,128]{1,0:T(8,128)(2,1)S(1)} %fusion.4.chooser_ref, ...), custom_call_target="tpu_custom_call" | custom-call | tf_op jit(solution)/shard_map/feed/pallas_call | solution.py:396
  98.3 1.9 %copy-done.1 = bf16[4096,512]{1,0:T(8,128)(2,1)} copy-done((bf16[4096,512]{1,0:T(8,128)(2,1)}, bf16[4096,512]{1,0:T(8,128)(2,1)S(1)}, u32[]{:S(2)}) %copy-start.1) | copy-done | bytes 4194328
  100.2 1.2 copy-done.4
  101.4 0.7 copy-done.7
  102.1 0.7 copy-done.9
  102.8 1.2 reshape.95.self_key_ref.self_value_ref
  104.0 1.0 reshape.94.masked_ref
  105.0 0.1 copy.16.owner_ref
  105.1 0.7 copy.17.length_ref
  105.8 1.4 copy-done.3
  107.2 1.4 copy-done.5
  108.7 48.7 %attend.1 = bf16[4,1536,128]{2,1,0:T(8,128)(2,1)S(1)} custom-call(bf16[1536,512]{1,0:T(8,128)(2,1)S(1)} %copy-done.5, bf16[192,512]{1,0:T(8,128)(2,1)S(1)} %reshape.94.masked_ref, bf16[4096,512]{1,0:T(8,128)(2,1)} %copy-done.1, bf16[12,128,512]{2,1,0:T(8,128)(2,1)S(1)} %copy-done.3, bf16[12,128,512]{2,1,0:T(8,128)(2,1)} %value_ref.1, ...), custom_call_target="tpu_custom_call" | custom-call | tf_op jit(solution)/shard_map/attend/pallas_call | solution.py:141
  157.4 1.8 %gather_fusion = bf16[128,4,8,128]{3,2,1,0:T(8,128)(2,1)} fusion(bf16[4,192,8,128]{3,2,1,0:T(8,128)(2,1)S(1)} %bitcast.25, s32[1024]{0:T(1024)S(1)} %pad_clamp_fusion), kind=kCustom, calls=%fused_computation | custom fusion | bytes 2097664 | tf_op jit(solution)/shard_map/gather | solution.py:492
  159.2 2.6 %copy.21 = bf16[16,8,32,128]{3,1,2,0:T(8,128)(2,1)} copy(bf16[16,8,32,128]{3,2,1,0:T(8,128)(2,1)} %bitcast.27) | data formatting | bytes 2097152
  (20 shorter events, 0.1 us)
Async XLA Ops:
  0.0 1.4 copy-start
  2.0 0.9 copy-start.11
  2.0 1.0 copy-start.12
  2.0 3.2 %copy-start.13 = (s32[128]{0:T(128)S(1)}, s32[128]{0:T(128)}, u32[]{:S(2)}) copy-start(s32[128]{0:T(128)} %param.18) | copy-start | bytes 1540
  2.4 2.9 %copy-start.6 = (bf16[512,512]{1,0:T(8,128)(2,1)S(1)}, bf16[512,512]{1,0:T(8,128)(2,1)}, u32[]{:S(2)}) copy-start(bf16[512,512]{1,0:T(8,128)(2,1)} %down_ref.1) | copy-start | bytes 1572868
  5.3 1.6 copy-start.2
  6.9 0.9 copy-start.8
  7.8 97.2 %copy-start.14 = (s32[16]{0:T(128)S(1)}, s32[16]{0:T(128)}, u32[]{:S(2)}) copy-start(s32[16]{0:T(128)} %param.19) | copy-start | bytes 196
  7.8 98.0 %copy-start.10 = (s32[16,12]{1,0:T(8,128)S(1)}, s32[16,12]{1,0:T(8,128)}, u32[]{:S(2)}) copy-start(s32[16,12]{1,0:T(8,128)} %table_ref.1) | copy-start | bytes 2308
  98.3 1.9 %copy-start.1 = (bf16[4096,512]{1,0:T(8,128)(2,1)}, bf16[4096,512]{1,0:T(8,128)(2,1)S(1)}, u32[]{:S(2)}) copy-start(bf16[4096,512]{1,0:T(8,128)(2,1)S(1)} %get-tuple-element.11.up_ref) | copy-start | bytes 12582916
  100.2 1.2 copy-start.4
  101.4 0.7 copy-start.7
  102.1 0.7 copy-start.9
  105.8 1.4 copy-start.3
  107.2 1.4 copy-start.5
